TPU v7x, 128 devices: a whole 4x4x4 slice. The times are simulated.
128 devices in a mesh: oi: 4 (over x), oj: 4 (over y_hi, core), vert: 8 (over y_lo, z).
Axes of the slice: x: 4, y: 4 (y_hi: 2, y_lo: 2; y = y_hi * 2 + y_lo), z: 4, core: 2. Of those that a mesh axis runs over, the one named last changes fastest.
Arguments:
- amps: bfloat16 [8192, 32768], P('oi', ('oj', 'vert')), may hold values from -6 to 6
- integrals: bfloat16 [32768, 4096], P(('oj', 'vert'), 'oi'), may hold values from -0.0625 to 0.0625
- amp_live: int32 [64, 256], P('oi', ('oj', 'vert')), may hold values 0 or 1
- int_live: int32 [256, 32], P(('oj', 'vert'), 'oi'), may hold values 0 or 1
- row_gap: float32 [8192], P('oi'), may hold values from 0.5 to 5
- col_gap: float32 [4096], P(('oj', 'vert')), may hold values from 0.5 to 5
Outputs:
- update: float32 [8192, 4096], P('oi', ('oj', 'vert'))
All inputs are finite; a program needn't handle non-finite values. No bound on the sum of `amp_live` or of `int_live` on one device may be relied on, other than what follows from the above.
Results may differ from a plain program's by a relative error of at most 0.0003.
Values may be sent and summed in bfloat16 or wider, within the bound.
No kernel may reach another device: no remote copies, remote signals or barrier semaphores. Data moves between devices by JAX's collectives and lax.ppermute only.
A program may use at most 128 MiB of HBM per device.

v0:
```python
import jax
import jax.numpy as jnp
from jax import lax
from jax.sharding import PartitionSpec as P


def mask_tiles(values, live):
    tile_rows, tile_cols = live.shape
    block = values.shape[0] // tile_rows
    shaped = values.reshape(tile_rows, block, tile_cols, values.shape[1] // tile_cols)
    kept = shaped * live.astype(values.dtype)[:, None, :, None]
    return kept.reshape(values.shape)


def per_device(amps, integrals, amp_live, int_live, row_gap, col_gap):
    amp_tiles = mask_tiles(amps, amp_live)
    int_tiles = mask_tiles(integrals, int_live)
    int_whole = lax.all_gather(int_tiles, "oi", axis=1, tiled=True)
    summed = lax.psum_scatter(
        lax.dot_general(
            int_whole, amp_tiles, (((0,), (1,)), ((), ())), preferred_element_type=jnp.float32
        ),
        ("oj", "vert"),
        scatter_dimension=0,
        tiled=True,
    )
    resid = summed.T
    return resid / (row_gap[:, None] + col_gap[None, :])


def solution(mesh):
    return jax.shard_map(
        per_device,
        mesh=mesh,
        in_specs=(
            P("oi", ("oj", "vert")),
            P(("oj", "vert"), "oi"),
            P("oi", ("oj", "vert")),
            P(("oj", "vert"), "oi"),
            P("oi"),
            P(("oj", "vert")),
        ),
        out_specs=P("oi", ("oj", "vert")),
        check_vma=False,
    )
```

profile of v0, /device:TPU:1, one launch (start us, length us, event | category | flops | bytes accessed | tf_op | source)
XLA Modules:
  0.0 497.1 jit_solution(10444352146463489243)
XLA Ops:
  6.5 0.0 all-gather.2.cloned.1.call-start
  6.5 0.7 convert_element_type.6
  7.2 0.3 mul.22
  7.6 0.0 copy-start.1
  7.6 3.2 bitcast_multiply_fusion.2
  10.8 0.0 all-gather.2.cloned.1.call-update
  10.8 0.0 reduce-scatter.2.cloned.1.call-start
  10.9 0.0 copy-done.1
  10.9 0.1 copy.7
  11.0 86.3 %all-gather.2.cloned.1.call-done = bf16[1024,4096]{1,0:T(8,128)(2,1)} async-done(((bf16[1024,1024]{1,0:T(8,128)(2,1)}), bf16[1024,4096]{1,0:T(8,128)(2,1)}) %all-gather.2.cloned.1.call-update) | async-done | bytes 8388624 | tf_op jit(solution)/shard_map/all_gather | solution.py:18
  97.3 0.6 mul.25
  97.9 25.5 %fusion = f32[4096,2048]{1,0:T(8,128)} fusion(bf16[1024,4096]{1,0:T(8,128)(2,1)} %all-gather.2.cloned.1.call-done, bf16[2048,1024]{1,0:T(8,128)(2,1)} %param.6, bf16[256,8,8,128]{3,2,1,0:T(8,128)(2,1)S(1)} %bitcast.13), kind=kOutput, calls=%fused_computation.1 | convolution fusion | flops 17181966336 | bytes 50331648 | tf_op jit(solution)/shard_map/dot_general | solution.py:20
  123.4 0.0 copy-start
  123.4 0.0 copy-start.2
  123.4 0.0 reduce-scatter.2.cloned.1.call-update
  123.4 364.1 %reduce-scatter.2.cloned.1.call-done = f32[128,2048]{1,0:T(8,128)} async-done(((f32[4096,2048]{1,0:T(8,128)}), f32[128,2048]{1,0:T(8,128)}) %reduce-scatter.2.cloned.1.call-update) | async-done | bytes 1048592 | tf_op jit(solution)/shard_map/reduce_scatter | solution.py:19
  487.6 0.0 copy-done
  487.6 0.0 copy-done.2
  487.6 1.4 bitcast_divide_fusion
  489.0 1.3 copy.8
  (1 shorter events, 0.0 us)
Async XLA Ops:
  6.5 90.7 %all-gather.2.cloned.1.call-start = ((), (), s32[]{:S(2)}) async-start(), calls=%async_computation.1 | async-start | bytes 10485760 | tf_op jit(solution)/shard_map/all_gather | solution.py:18
  7.6 3.3 copy-start.1
  10.8 476.7 %reduce-scatter.2.cloned.1.call-start = ((), (), s32[]{:S(2)}) async-start(), calls=%async_computation.2 | async-start | bytes 34603008 | tf_op jit(solution)/shard_map/reduce_scatter | solution.py:19
  123.4 364.1 %copy-start = (f32[2048]{0:T(1024)S(1)}, f32[2048]{0:T(1024)}, u32[]{:S(2)}) copy-start(f32[2048]{0:T(1024)} %param.10) | copy-start | bytes 24580
  123.4 364.1 %copy-start.2 = (f32[128]{0:T(128)S(1)}, f32[128]{0:T(128)}, u32[]{:S(2)}) copy-start(f32[128]{0:T(128)} %param.11) | copy-start | bytes 1540
Sparse Core Ops, SparseCore 0:
  11.0 86.2 all-gather.1
  123.6 363.9 reduce-scatter.1
where the time goes:
time: 497 us
  waiting for transfers between devices  450 us (91%)
  matrix products  25.5 us (5%)
  between operations  13.4 us (3%)
  other arithmetic  5.35 us (1%)
    reduce_scatter x1, waiting for transfers between devices, per_device(): lax.psum_scatter(lax.dot_general(int_whole, amp_tiles, (((0,), (1,)), (()...  364 us
    all_gather x1, waiting for transfers between devices, per_device(): int_whole = lax.all_gather(int_tiles, 'oi', axis=1, tiled=True)  86.3 us
    dot_general x1, matrix products, per_device(): lax.dot_general(int_whole, amp_tiles, (((0,), (1,)), ((), ())), preferred...  25.5 us
  transfers between devices with their start and end apart: 2, of which 2 were waited for; matrix products, arithmetic and copies ran while one was open for 0% of the time, Pallas kernels for 0%

commit v1 on v0

v1 whole, which is shorter than its diff:
```python
import functools
import jax
import jax.numpy as jnp
from jax import lax
from jax.experimental import pallas as pl
from jax.experimental.pallas import tpu as pltpu
from jax.sharding import PartitionSpec as P

AXES = ("oi", "oj", "vert")
SIDE = 4
LANES = 128
LANE_TILE = 512
TOP = 32512.0
STEPS_PER_OCTAVE = 64.0
VMEM_BYTES = 40 * 1024 * 1024


def place_of(i):
    x, rest = divmod(i, 32)
    y_hi, rest = divmod(rest, 16)
    core, rest = divmod(rest, 8)
    y_lo, z = divmod(rest, 4)
    return x, 2 * y_hi + y_lo, z, core


def index_in_plane(y, z, core):
    y, z = y % SIDE, z % SIDE
    return (((y // 2) * 2 + core) * 2 + y % 2) * 4 + z


def shift(value, dx=0, dy=0, dz=0, dcore=0):
    pairs = []
    for i in range(128):
        x, y, z, core = place_of(i)
        pairs.append((i, (x + dx) % SIDE * 32 + index_in_plane(y + dy, z + dz, (core + dcore) % 2)))
    return lax.ppermute(value, AXES, pairs)


def mask_tiles(values, live):
    tile_rows, tile_cols = live.shape
    block = values.shape[0] // tile_rows
    shaped = values.reshape(tile_rows, block, tile_cols, values.shape[1] // tile_cols)
    kept = shaped * live.astype(values.dtype)[:, None, :, None]
    return kept.reshape(values.shape)


def lane_index(rows):
    return lax.broadcasted_iota(jnp.int32, (rows, LANES), 1)


def store_codes(out, rows, lanes_at, tile, values):
    peak = jnp.maximum(jnp.max(jnp.abs(values), axis=1, keepdims=True), 1e-30)
    code = jnp.ceil(jnp.log2(peak) * STEPS_PER_OCTAVE)
    steps = jnp.round(values * (jnp.exp2(code * (-1.0 / STEPS_PER_OCTAVE)) * TOP))
    out[rows, pl.ds(lanes_at, LANE_TILE)] = steps.astype(jnp.int32).astype(jnp.int16)
    return code


def load_codes(ref, rows, tile):
    heads = ref[rows, pl.ds(ref.shape[1] - LANES, LANES)].astype(jnp.int32)
    code = jnp.sum(jnp.where(lane_index(heads.shape[0]) == tile, heads, 0), axis=1, keepdims=True)
    scale = jnp.exp2(code.astype(jnp.float32) * (1.0 / STEPS_PER_OCTAVE)) * (1.0 / TOP)
    return ref[rows, pl.ds(tile * LANE_TILE, LANE_TILE)].astype(jnp.int32).astype(jnp.float32) * scale


def store_heads(out, rows, n_rows, codes):
    lane = lane_index(n_rows)
    heads = jnp.zeros((n_rows, LANES), jnp.int32)
    for tile, code in codes:
        heads = jnp.where(lane == tile, code.astype(jnp.int32), heads)
    out[rows, pl.ds(out.shape[1] - LANES, LANES)] = heads.astype(jnp.int16)


def rows_of(order, n, at):
    if order == "z":
        return [pl.ds(pl.multiple_of((q * 4 + at) * n, 16), n) for q in range(4)]
    return [pl.ds(pl.multiple_of(at * 4 * n, 16), 4 * n)]


def product_kernel(order, n, n_pieces, table, *refs):
    pieces, (a_own, a_other), rest = refs[:n_pieces], refs[n_pieces:n_pieces + 2], refs[n_pieces + 2:]
    acc, outs = rest[-1], rest[:-1]
    tile = pl.program_id(0)
    depth = a_own.shape[0]
    at = 0
    for piece in pieces:
        m = piece.shape[0]
        acc[pl.ds(at, m), :] = jnp.dot(
            piece[:, pl.ds(0, depth)], a_own[...], preferred_element_type=jnp.float32
        ) + jnp.dot(piece[:, pl.ds(depth, depth)], a_other[...], preferred_element_type=jnp.float32)
        at += m
    lanes_at = pl.multiple_of(tile * LANE_TILE, LANE_TILE)

    def coded(out, into, source):
        code = store_codes(out, into, lanes_at, tile, acc[source, :])
        size = into.size
        heads_at = (into, pl.ds(out.shape[1] - LANES, LANES))
        before = jnp.where(tile == 0, 0, out[heads_at].astype(jnp.int32))
        out[heads_at] = jnp.where(lane_index(size) == tile, code.astype(jnp.int32), before).astype(jnp.int16)

    if order == "all":
        for y in range(4):
            coded(outs[0], pl.ds(y * 4 * n, 4 * n), rows_of("y", n, table[y])[0])
        return
    for to, out in enumerate(outs):
        row = 0
        for source in rows_of(order, n, table[to]):
            into = pl.ds(row, source.size)
            if to == 0:
                out[into, pl.ds(lanes_at, LANE_TILE)] = acc[source, :]
            else:
                coded(out, into, source)
            row += source.size


def products(order, n, table, pieces, a_own, a_other):
    depth, rows = a_own.shape
    if order == "all":
        out_shape = [jax.ShapeDtypeStruct((16 * n, rows + LANES), jnp.int16)]
    else:
        out_shape = [jax.ShapeDtypeStruct((4 * n, rows), jnp.float32)] + [
            jax.ShapeDtypeStruct((4 * n, rows + LANES), jnp.int16)
        ] * 3
    whole = lambda shape: pl.BlockSpec(shape, lambda j, t: (0, 0))
    flops = 2 * 16 * n * 2 * depth * rows
    moved = 16 * n * 4 * depth + 4 * depth * rows + 10 * n * rows * 2
    return pl.pallas_call(
        functools.partial(product_kernel, order, n, len(pieces)),
        out_shape=out_shape,
        grid_spec=pltpu.PrefetchScalarGridSpec(
            num_scalar_prefetch=1,
            grid=(rows // LANE_TILE,),
            in_specs=[whole(p.shape) for p in pieces]
            + [pl.BlockSpec((depth, LANE_TILE), lambda j, t: (0, j))] * 2,
            out_specs=[whole(s.shape) for s in out_shape],
            scratch_shapes=[pltpu.VMEM((16 * n, LANE_TILE), jnp.float32)],
        ),
        compiler_params=pltpu.CompilerParams(vmem_limit_bytes=VMEM_BYTES),
        cost_estimate=pl.CostEstimate(flops=flops, bytes_accessed=moved, transcendentals=0),
    )(table, *pieces, a_own, a_other)


def join_kernel(n, table, kept, one, two, three, *outs_and_scratch):
    *outs, total = outs_and_scratch
    rows = kept.shape[0]
    tiles = kept.shape[1] // LANE_TILE
    everything = pl.ds(0, rows)
    codes = [[] for _ in outs]
    for tile in range(tiles):
        lanes = pl.ds(tile * LANE_TILE, LANE_TILE)
        total[...] = kept[:, lanes] + sum(load_codes(ref, everything, tile) for ref in (one, two, three))
        for to, out in enumerate(outs):
            source = total[pl.ds(pl.multiple_of(table[to] * n, 16), n), :]
            if to == 0:
                out[:, lanes] = source
            else:
                codes[to].append((tile, store_codes(out, pl.ds(0, n), tile * LANE_TILE, tile, source)))
    for to in range(1, len(outs)):
        store_heads(outs[to], pl.ds(0, n), n, codes[to])


def join(n, table, kept, arrived):
    rows = kept.shape[1]
    out_shape = [jax.ShapeDtypeStruct((n, rows), jnp.float32)] + [
        jax.ShapeDtypeStruct((n, rows + LANES), jnp.int16)
    ] * 3
    vmem = pl.BlockSpec(memory_space=pltpu.VMEM)
    return pl.pallas_call(
        functools.partial(join_kernel, n),
        out_shape=out_shape,
        in_specs=[pl.BlockSpec(memory_space=pltpu.SMEM)] + [vmem] * 4,
        out_specs=[vmem] * 4,
        scratch_shapes=[pltpu.VMEM((4 * n, LANE_TILE), jnp.float32)],
        compiler_params=pltpu.CompilerParams(vmem_limit_bytes=VMEM_BYTES),
        cost_estimate=pl.CostEstimate(flops=40 * n * rows, bytes_accessed=50 * n * rows, transcendentals=0),
    )(table, kept, *arrived)


def last_kernel(kept, one, two, three, out):
    everything = pl.ds(0, kept.shape[0])
    for tile in range(kept.shape[1] // LANE_TILE):
        lanes = pl.ds(tile * LANE_TILE, LANE_TILE)
        out[:, lanes] = kept[:, lanes] + sum(load_codes(ref, everything, tile) for ref in (one, two, three))


def last(kept, arrived):
    vmem = pl.BlockSpec(memory_space=pltpu.VMEM)
    return pl.pallas_call(
        last_kernel,
        out_shape=jax.ShapeDtypeStruct(kept.shape, jnp.float32),
        in_specs=[vmem] * 4,
        out_specs=vmem,
        compiler_params=pltpu.CompilerParams(vmem_limit_bytes=VMEM_BYTES),
        cost_estimate=pl.CostEstimate(flops=10 * kept.size, bytes_accessed=14 * kept.size, transcendentals=0),
    )(kept, *arrived)


def sum_kernel(n, arrived, out):
    for tile in range(out.shape[1] // LANE_TILE):
        out[:, pl.ds(tile * LANE_TILE, LANE_TILE)] = sum(
            load_codes(arrived, pl.ds(k * n, n), tile) for k in range(16)
        )


def sum_of(n, arrived):
    rows = arrived.shape[1] - LANES
    vmem = pl.BlockSpec(memory_space=pltpu.VMEM)
    return pl.pallas_call(
        functools.partial(sum_kernel, n),
        out_shape=jax.ShapeDtypeStruct((n, rows), jnp.float32),
        in_specs=[vmem],
        out_specs=vmem,
        compiler_params=pltpu.CompilerParams(vmem_limit_bytes=VMEM_BYTES),
        cost_estimate=pl.CostEstimate(flops=50 * n * rows, bytes_accessed=36 * n * rows, transcendentals=0),
    )(arrived)


PLANE_GROUPS = [[index_in_plane(y, z, core) for y in range(4) for z in range(4)] for core in range(2)]
CHUNKS = (32, 32)
ORDERS_NEAR = ("z", "y")
ORDERS_FAR = ("z", "all")


def per_device(amps, integrals, amp_live, int_live, row_gap, col_gap):
    x = lax.axis_index("oi")
    oj, vert = lax.axis_index("oj"), lax.axis_index("vert")
    core, y, z = oj % 2, (oj // 2) * 2 + vert // 4, vert % 4
    around = jnp.arange(4, dtype=jnp.int32)

    int_t = mask_tiles(integrals, int_live).T.reshape(8, 2, 64, integrals.shape[0])
    mine = lax.dynamic_index_in_dim(int_t, core, 1, keepdims=False)
    theirs = lax.dynamic_index_in_dim(int_t, 1 - core, 1, keepdims=False)
    both = jnp.concatenate([mine, shift(theirs, dcore=1)], axis=2)
    a_own = mask_tiles(amps, amp_live).T
    a_other = shift(a_own, dcore=1)

    def y_table(first_block, places):
        pair = jnp.where(places // 2 == (first_block % 4) // 2, 0, 1)
        return (pair * 2 + places % 2).astype(jnp.int32)

    def spread(order, n, first_block, pieces):
        if order == "all":
            (sent,) = products(order, n, y_table(first_block, around), pieces, a_own, a_other)
            got = lax.all_to_all(sent, ("oj", "vert"), 0, 0, axis_index_groups=PLANE_GROUPS, tiled=True)
            return sum_of(n, got)
        z_rel, y_rel = ((z + around) % 4).astype(jnp.int32), y_table(first_block, (y + around) % 4)
        along_z = [functools.partial(shift, dz=d) for d in (1, 2, 3)]
        along_y = [functools.partial(shift, dy=d) for d in (1, 2, 3)]
        steps = [(z_rel, along_z), (y_rel, along_y)]
        if order == "y":
            steps = steps[::-1]
        kept, *sent = products(order, n, steps[0][0], pieces, a_own, a_other)
        arrived = [go(s) for go, s in zip(steps[0][1], sent)]
        kept, *sent = join(n, steps[1][0], kept, arrived)
        return last(kept, [go(s) for go, s in zip(steps[1][1], sent)])

    near, far = [], []
    offset = 0
    own, left, right = [], [], []
    for n in CHUNKS:
        own.append(both[:, offset:offset + n].reshape(8 * n, both.shape[2]))
        offset += n
        left.append(shift(own[-1], dx=1))
        right.append(shift(own[-1], dx=-1))
    for j, n in enumerate(CHUNKS):
        near.append(spread(ORDERS_NEAR[j], n, x - 1, [left[j], right[j]]))
        low = shift(left[j][:4 * n], dx=1)
        high = shift(right[j][4 * n:], dx=-1)
        far.append(spread(ORDERS_FAR[j], n, x, [own[j], low, high]))
    near, far = jnp.concatenate(near), jnp.concatenate(far)
    far_is_mine = core == x % 2
    kept = jnp.where(far_is_mine, far, near)
    swapped = shift(jnp.where(far_is_mine, near, far), dcore=1)
    resid = jnp.where(core == 0, jnp.concatenate([kept, swapped]), jnp.concatenate([swapped, kept])).T
    return resid / (row_gap[:, None] + col_gap[None, :])


def solution(mesh):
    return jax.shard_map(
        per_device,
        mesh=mesh,
        in_specs=(
            P("oi", ("oj", "vert")),
            P(("oj", "vert"), "oi"),
            P("oi", ("oj", "vert")),
            P(("oj", "vert"), "oi"),
            P("oi"),
            P(("oj", "vert")),
        ),
        out_specs=P("oi", ("oj", "vert")),
        check_vma=False,
    )
```

time: 497 us -> 217 us (0.44)
  waiting for transfers between devices: 450 us -> 76.9 us
  starting transfers between devices: 0.04 us -> 59.4 us
  Pallas kernels: 0 us -> 45.4 us
  local copies, waits for them, and re-layouts: 2.35 us -> 30 us
  matrix products: 25.5 us -> 0 us
  between operations: 13.4 us -> 0.32 us
    reduce_scatter x1 -> x0, waiting for transfers between devices: 364 us -> none  [per_device(): lax.psum_scatter(lax.dot_general(int_whole, amp_tiles, (((0,), (1,)), (()...]
    all_gather x1 -> x0, waiting for transfers between devices: 86.3 us -> none  [per_device(): int_whole = lax.all_gather(int_tiles, 'oi', axis=1, tiled=True)]
    ppermute x0 -> x29, waiting for transfers between devices: none -> 76.9 us  [shift(): return lax.ppermute(value, AXES, pairs)]
    ppermute x0 -> x29, starting transfers between devices: none -> 51.5 us  [shift(): return lax.ppermute(value, AXES, pairs)]
    pallas_call x0 -> x11, Pallas kernels: none -> 45.4 us  [the longest x4 34.7 us: products(): pl.pallas_call(functools.partial(product_kernel, order, n, len(pieces)),...]
    dot_general x1 -> x0, matrix products: 25.5 us -> none  [per_device(): lax.dot_general(int_whole, amp_tiles, (((0,), (1,)), ((), ())), preferred...]
    unnamed x6 -> x44, local copies, waits for them, and re-layouts: 0.01 us -> 23.1 us
    all_to_all x0 -> x1, starting transfers between devices: none -> 7.85 us  [spread(): lax.all_to_all(sent, ('oj', 'vert'), 0, 0, axis_index_groups=PLANE_GROUPS...]
  transfers between devices with their start and end apart: 2 -> 30, of which waited for: 2 -> 9; matrix products, arithmetic and copies ran while one was open for 0% -> 4% of each run, Pallas kernels for 0% -> 21%
where the time goes in v1:
time: 217 us
  waiting for transfers between devices  76.9 us (35%)
  starting transfers between devices  59.4 us (27%)
  Pallas kernels  45.4 us (21%)
  local copies, waits for them, and re-layouts  30 us (14%)
  other arithmetic  4.45 us (2%)
    ppermute x29, waiting for transfers between devices, shift(): return lax.ppermute(value, AXES, pairs)  76.9 us
    ppermute x29, starting transfers between devices, shift(): return lax.ppermute(value, AXES, pairs)  51.5 us
    pallas_call x4, Pallas kernels, products(): pl.pallas_call(functools.partial(product_kernel, order, n, len(pieces)),...  34.7 us
    unnamed x44, local copies, waits for them, and re-layouts  23.1 us
    all_to_all x1, starting transfers between devices, spread(): lax.all_to_all(sent, ('oj', 'vert'), 0, 0, axis_index_groups=PLANE_GROUPS...  7.85 us
    pallas_call x3, Pallas kernels, join(): pl.pallas_call(functools.partial(join_kernel, n), out_shape=out_shape, in...  6.99 us
  transfers between devices with their start and end apart: 30, of which 9 were waited for; matrix products, arithmetic and copies ran while one was open for 4% of the time, Pallas kernels for 21%

profile of v1, /device:TPU:1, one launch (start us, length us, event | category | flops | bytes accessed | tf_op | source)
XLA Modules:
  0.0 216.5 jit_solution(12640923163089630864)
XLA Ops:
  0.7 6.5 %copy.13 = bf16[2048,1024]{0,1:T(8,128)(2,1)} copy(bf16[2048,1024]{1,0:T(8,128)(2,1)} %param.6) | data formatting | bytes 8388608 | tf_op args[0]
  9.4 2.9 %fusion.refs_3_.refs_2_ = bf16[1024,2048]{1,0:T(8,128)(2,1)} fusion(bf16[2048,1024]{0,1:T(8,128)(2,1)S(1)} %copy-done.17, bf16[128,8,16,128]{3,2,1,0:T(8,128)(2,1)S(1)} %bitcast.39), kind=kLoop, calls=%fused_computation.1 | loop fusion | flops 2097152 | bytes 12582912 | tf_op jit(solution)/shard_map/transpose | solution.py:234
  13.8 2.9 %copy.12 = bf16[1024,1024]{0,1:T(8,128)(2,1)S(1)} copy(bf16[1024,1024]{1,0:T(8,128)(2,1)} %param.7) | data formatting | bytes 4194304 | tf_op args[1]
  17.6 4.4 %collective-permute-done = bf16[8,64,1024]{2,1,0:T(8,128)(2,1)S(1)} collective-permute-done((bf16[8,64,1024]{2,1,0:T(8,128)(2,1)S(1)}, bf16[8,64,1024]{2,1,0:T(8,128)(2,1)S(1)}, u32[]{:S(2)}, u32[]{:S(2)}) %collective-permute-start) | collective-permute-done | bytes 1048608 | tf_op jit(solution)/shard_map/ppermute | solution.py:36
  25.0 2.6 %collective-permute-start.3 = (bf16[256,2048]{1,0:T(8,128)(2,1)S(1)}, bf16[256,2048]{1,0:T(8,128)(2,1)}, u32[]{:S(2)}, u32[]{:S(2)}) collective-permute-start(bf16[256,2048]{1,0:T(8,128)(2,1)S(1)} %bitcast.34), channel_id=1, source_target_pairs={{0,96},{1,97},{2,98},{3,99},{4,100},{5,101},{6,102},{7,103},{8,104... | collective-permute-start | bytes 3145736 | tf_op jit(solution)/shard_map/ppermute | solution.py:36
  27.6 20.2 %collective-permute-done.12.refs_0_ = bf16[256,2048]{1,0:T(8,128)(2,1)S(1)} collective-permute-done((bf16[256,2048]{1,0:T(8,128)(2,1)S(1)}, bf16[256,2048]{1,0:T(8,128)(2,1)S(1)}, u32[]{:S(2)}, u32[]{:S(2)}) %collective-permute-start.12) | collective-permute-done | bytes 1048608 | tf_op jit(solution)/shard_map/ppermute | solution.py:36
  51.6 2.6 %collective-permute-start.15 = (bf16[128,2048]{1,0:T(8,128)(2,1)}, bf16[128,2048]{1,0:T(8,128)(2,1)}, u32[]{:S(2)}, u32[]{:S(2)}) collective-permute-start(bf16[128,2048]{1,0:T(8,128)(2,1)} %slice.29), channel_id=1, source_target_pairs={{0,96},{1,97},{2,98},{3,99},{4,100},{5,101},{6,102},{7,103},{8,104... | collective-permute-start | bytes 1572872 | tf_op jit(solution)/shard_map/ppermute | solution.py:36
  54.1 16.1 %collective-permute-done.1.refs_0_ = bf16[256,2048]{1,0:T(8,128)(2,1)S(1)} collective-permute-done((bf16[256,2048]{1,0:T(8,128)(2,1)S(1)}, bf16[256,2048]{1,0:T(8,128)(2,1)S(1)}, u32[]{:S(2)}, u32[]{:S(2)}) %collective-permute-start.1) | collective-permute-done | bytes 1048608 | tf_op jit(solution)/shard_map/ppermute | solution.py:36
  73.3 2.5 %collective-permute-start.4 = (bf16[128,2048]{1,0:T(8,128)(2,1)}, bf16[128,2048]{1,0:T(8,128)(2,1)}, u32[]{:S(2)}, u32[]{:S(2)}) collective-permute-start(bf16[128,2048]{1,0:T(8,128)(2,1)} %slice.27), channel_id=1, source_target_pairs={{0,96},{1,97},{2,98},{3,99},{4,100},{5,101},{6,102},{7,103},{8,104... | collective-permute-start | bytes 1572872 | tf_op jit(solution)/shard_map/ppermute | solution.py:36
  75.8 5.8 %collective-permute-done.13.refs_1_ = bf16[128,2048]{1,0:T(8,128)(2,1)} collective-permute-done((bf16[128,2048]{1,0:T(8,128)(2,1)}, bf16[128,2048]{1,0:T(8,128)(2,1)}, u32[]{:S(2)}, u32[]{:S(2)}) %collective-permute-start.13) | collective-permute-done | bytes 524320 | tf_op jit(solution)/shard_map/ppermute | solution.py:36
  81.6 8.8 %shard_map.67 = s16[512,2176]{1,0:T(8,128)(2,1)S(1)} custom-call(s32[4]{0:T(128)S(1)} %fusion.6.table, bf16[256,2048]{1,0:T(8,128)(2,1)S(1)} %bitcast.38, bf16[128,2048]{1,0:T(8,128)(2,1)} %collective-permute-done.13.refs_1_, bf16[128,2048]{1,0:T(8,128)(2,1)} %collective-permute-done.15.refs_2_, bf16[1024,2048]{1,0:T(8,128)(2,1)} %fusion.refs_3_.refs_2_, ...), custom_call_target="tpu_custom_call" | custom-call | flops 4294967296 | bytes 11796480 | tf_op jit(solution)/shard_map/pallas_call | solution.py:127
  91.8 7.8 %all-to-all-start = ((s16[16,32,2176]{2,1,0:T(8,128)(2,1)}), s16[16,32,2176]{2,1,0:T(8,128)(2,1)S(1)}, u32[]{:S(2)}, u32[]{:S(2)}) async-start(s16[16,32,2176]{2,1,0:T(8,128)(2,1)} %bitcast.32), calls=%async_computation | async-start | bytes 4456448 | tf_op jit(solution)/shard_map/all_to_all | solution.py:244
  100.9 9.3 %shard_map.64 = (f32[128,2048]{1,0:T(8,128)S(1)}, s16[128,2176]{1,0:T(8,128)(2,1)}, s16[128,2176]{1,0:T(8,128)(2,1)S(1)}, s16[128,2176]{1,0:T(8,128)(2,1)S(1)}) custom-call(s32[4]{0:T(128)S(1)} %and_select_fusion.2.table, bf16[256,2048]{1,0:T(8,128)(2,1)S(1)} %bitcast.35, bf16[128,2048]{1,0:T(8,128)(2,1)} %collective-permute-done.2.refs_1_, ...), custom_call_target="tpu_custom_call" | custom-call | flops 4294967296 | bytes 11796480 | tf_op jit(solution)/shard_map/pallas_call | solution.py:127
  118.0 8.5 %shard_map.69 = (f32[128,2048]{1,0:T(8,128)S(1)}, s16[128,2176]{1,0:T(8,128)(2,1)S(1)}, s16[128,2176]{1,0:T(8,128)(2,1)S(1)}, s16[128,2176]{1,0:T(8,128)(2,1)S(1)}) custom-call(s32[4]{0:T(128)S(1)} %and_select_fusion.2.table, bf16[256,2048]{1,0:T(8,128)(2,1)S(1)} %copy-done.8, bf16[256,2048]{1,0:T(8,128)(2,1)} %collective-permute-done.3.refs_1_, ...), custom_call_target="tpu_custom_call" | custom-call | flops 4294967296 | bytes 11796480 | tf_op jit(solution)/shard_map/pallas_call | solution.py:127
  128.2 11.3 %collective-permute-done.6.one = s16[128,2176]{1,0:T(8,128)(2,1)} collective-permute-done((s16[128,2176]{1,0:T(8,128)(2,1)}, s16[128,2176]{1,0:T(8,128)(2,1)}, u32[]{:S(2)}, u32[]{:S(2)}) %collective-permute-start.6) | collective-permute-done | bytes 557088 | tf_op jit(solution)/shard_map/ppermute | solution.py:36
  139.5 8.2 %shard_map.72 = (f32[128,2048]{1,0:T(8,128)S(1)}, s16[128,2176]{1,0:T(8,128)(2,1)S(1)}, s16[128,2176]{1,0:T(8,128)(2,1)S(1)}, s16[128,2176]{1,0:T(8,128)(2,1)S(1)}) custom-call(s32[4]{0:T(128)S(1)} %fusion.11.table, bf16[256,2048]{1,0:T(8,128)(2,1)S(1)} %copy-done.4, bf16[256,2048]{1,0:T(8,128)(2,1)S(1)} %copy-done.6, ...), custom_call_target="tpu_custom_call" | custom-call | flops 4294967296 | bytes 11796480 | tf_op jit(solution)/shard_map/pallas_call | solution.py:127
  147.7 2.9 %collective-permute-done.7.two = s16[128,2176]{1,0:T(8,128)(2,1)S(1)} collective-permute-done((s16[128,2176]{1,0:T(8,128)(2,1)}, s16[128,2176]{1,0:T(8,128)(2,1)S(1)}, u32[]{:S(2)}, u32[]{:S(2)}) %collective-permute-start.7) | collective-permute-done | bytes 557088 | tf_op jit(solution)/shard_map/ppermute | solution.py:36
  152.6 2.9 %collective-permute-start.23 = (s16[128,2176]{1,0:T(8,128)(2,1)S(1)}, s16[128,2176]{1,0:T(8,128)(2,1)S(1)}, u32[]{:S(2)}, u32[]{:S(2)}) collective-permute-start(s16[128,2176]{1,0:T(8,128)(2,1)S(1)} %get-tuple-element.47), channel_id=1, source_target_pairs={{0,16},{1,17},{2,18},{3,19},{4,20},{5,21},{6,22},{7,23},{8,24},{9,... | collective-permute-start | bytes 1671176 | tf_op jit(solution)/shard_map/ppermute | solution.py:36
  155.5 7.7 %collective-permute-done.16.one = s16[128,2176]{1,0:T(8,128)(2,1)S(1)} collective-permute-done((s16[128,2176]{1,0:T(8,128)(2,1)S(1)}, s16[128,2176]{1,0:T(8,128)(2,1)S(1)}, u32[]{:S(2)}, u32[]{:S(2)}) %collective-permute-start.16) | collective-permute-done | bytes 557088 | tf_op jit(solution)/shard_map/ppermute | solution.py:36
  167.5 6.9 %collective-permute-done.17.two = s16[128,2176]{1,0:T(8,128)(2,1)S(1)} collective-permute-done((s16[128,2176]{1,0:T(8,128)(2,1)S(1)}, s16[128,2176]{1,0:T(8,128)(2,1)S(1)}, u32[]{:S(2)}, u32[]{:S(2)}) %collective-permute-start.17) | collective-permute-done | bytes 557088 | tf_op jit(solution)/shard_map/ppermute | solution.py:36
  182.6 2.7 %collective-permute-start.20 = (s16[32,2176]{1,0:T(8,128)(2,1)}, s16[32,2176]{1,0:T(8,128)(2,1)}, u32[]{:S(2)}, u32[]{:S(2)}) collective-permute-start(s16[32,2176]{1,0:T(8,128)(2,1)} %get-tuple-element.43), channel_id=1, source_target_pairs={{0,16},{1,17},{2,18},{3,19},{4,20},{5,21},{6,22},{7,23},{8,24},{9,... | collective-permute-start | bytes 417800 | tf_op jit(solution)/shard_map/ppermute | solution.py:36
  187.8 2.8 %collective-permute-start.21 = (s16[32,2176]{1,0:T(8,128)(2,1)}, s16[32,2176]{1,0:T(8,128)(2,1)}, u32[]{:S(2)}, u32[]{:S(2)}) collective-permute-start(s16[32,2176]{1,0:T(8,128)(2,1)} %get-tuple-element.44), channel_id=1, source_target_pairs={{0,20},{1,21},{2,22},{3,23},{4,0},{5,1},{6,2},{7,3},{8,28},{9,29},... | collective-permute-start | bytes 417800 | tf_op jit(solution)/shard_map/ppermute | solution.py:36
  191.2 8.0 %collective-permute-start.25 = (s16[32,2176]{1,0:T(8,128)(2,1)}, s16[32,2176]{1,0:T(8,128)(2,1)}, u32[]{:S(2)}, u32[]{:S(2)}) collective-permute-start(s16[32,2176]{1,0:T(8,128)(2,1)} %get-tuple-element.50), channel_id=1, source_target_pairs={{0,1},{1,2},{2,3},{3,0},{4,5},{5,6},{6,7},{7,4},{8,9},{9,10},{10,1... | collective-permute-start | bytes 417800 | tf_op jit(solution)/shard_map/ppermute | solution.py:36
  209.6 3.9 %collective-permute-start.28 = (f32[64,2048]{1,0:T(8,128)S(1)}, f32[64,2048]{1,0:T(8,128)S(1)}, u32[]{:S(2)}, u32[]{:S(2)}) collective-permute-start(f32[64,2048]{1,0:T(8,128)S(1)} %get-tuple-element.58), channel_id=1, source_target_pairs={{0,8},{1,9},{2,10},{3,11},{4,12},{5,13},{6,14},{7,15},{8,0},{9,1},... | collective-permute-start | bytes 1572872 | tf_op jit(solution)/shard_map/ppermute | solution.py:36
  (111 shorter events, 58.1 us)
Async XLA Ops:
  12.3 69.3 %collective-permute-start.5 = (bf16[1024,2048]{1,0:T(8,128)(2,1)}, bf16[1024,2048]{1,0:T(8,128)(2,1)}, u32[]{:S(2)}, u32[]{:S(2)}) collective-permute-start(bf16[1024,2048]{1,0:T(8,128)(2,1)} %fusion.refs_3_.refs_2_), channel_id=1, source_target_pairs={{0,8},{1,9},{2,10},{3,11},{4,12},{5,13},{6,14},{7,15},{8,0},{9,1},... | collective-permute-start | bytes 12582920 | tf_op jit(solution)/shard_map/ppermute | solution.py:36
  22.2 25.7 %collective-permute-start.12 = (bf16[256,2048]{1,0:T(8,128)(2,1)S(1)}, bf16[256,2048]{1,0:T(8,128)(2,1)S(1)}, u32[]{:S(2)}, u32[]{:S(2)}) collective-permute-start(bf16[256,2048]{1,0:T(8,128)(2,1)S(1)} %bitcast.36), channel_id=1, source_target_pairs={{0,32},{1,33},{2,34},{3,35},{4,36},{5,37},{6,38},{7,39},{8,40},{9,... | collective-permute-start | bytes 3145736 | tf_op jit(solution)/shard_map/ppermute | solution.py:36
  23.5 26.2 %collective-permute-start.14 = (bf16[256,2048]{1,0:T(8,128)(2,1)S(1)}, bf16[256,2048]{1,0:T(8,128)(2,1)S(1)}, u32[]{:S(2)}, u32[]{:S(2)}) collective-permute-start(bf16[256,2048]{1,0:T(8,128)(2,1)S(1)} %bitcast.37), channel_id=1, source_target_pairs={{0,96},{1,97},{2,98},{3,99},{4,100},{5,101},{6,102},{7,103},{8,104... | collective-permute-start | bytes 3145736 | tf_op jit(solution)/shard_map/ppermute | solution.py:36
  24.9 45.4 %collective-permute-start.1 = (bf16[256,2048]{1,0:T(8,128)(2,1)S(1)}, bf16[256,2048]{1,0:T(8,128)(2,1)S(1)}, u32[]{:S(2)}, u32[]{:S(2)}) collective-permute-start(bf16[256,2048]{1,0:T(8,128)(2,1)S(1)} %bitcast.33), channel_id=1, source_target_pairs={{0,32},{1,33},{2,34},{3,35},{4,36},{5,37},{6,38},{7,39},{8,40},{9,... | collective-permute-start | bytes 3145736 | tf_op jit(solution)/shard_map/ppermute | solution.py:36
  25.0 46.4 %collective-permute-start.3 = (bf16[256,2048]{1,0:T(8,128)(2,1)S(1)}, bf16[256,2048]{1,0:T(8,128)(2,1)}, u32[]{:S(2)}, u32[]{:S(2)}) collective-permute-start(bf16[256,2048]{1,0:T(8,128)(2,1)S(1)} %bitcast.34), channel_id=1, source_target_pairs={{0,96},{1,97},{2,98},{3,99},{4,100},{5,101},{6,102},{7,103},{8,104... | collective-permute-start | bytes 3145736 | tf_op jit(solution)/shard_map/ppermute | solution.py:36
  49.6 32.0 %collective-permute-start.13 = (bf16[128,2048]{1,0:T(8,128)(2,1)}, bf16[128,2048]{1,0:T(8,128)(2,1)}, u32[]{:S(2)}, u32[]{:S(2)}) collective-permute-start(bf16[128,2048]{1,0:T(8,128)(2,1)} %slice.28), channel_id=1, source_target_pairs={{0,32},{1,33},{2,34},{3,35},{4,36},{5,37},{6,38},{7,39},{8,40},{9,... | collective-permute-start | bytes 1572872 | tf_op jit(solution)/shard_map/ppermute | solution.py:36
  51.6 30.1 %collective-permute-start.15 = (bf16[128,2048]{1,0:T(8,128)(2,1)}, bf16[128,2048]{1,0:T(8,128)(2,1)}, u32[]{:S(2)}, u32[]{:S(2)}) collective-permute-start(bf16[128,2048]{1,0:T(8,128)(2,1)} %slice.29), channel_id=1, source_target_pairs={{0,96},{1,97},{2,98},{3,99},{4,100},{5,101},{6,102},{7,103},{8,104... | collective-permute-start | bytes 1572872 | tf_op jit(solution)/shard_map/ppermute | solution.py:36
  71.2 28.5 %collective-permute-start.2 = (bf16[128,2048]{1,0:T(8,128)(2,1)}, bf16[128,2048]{1,0:T(8,128)(2,1)}, u32[]{:S(2)}, u32[]{:S(2)}) collective-permute-start(bf16[128,2048]{1,0:T(8,128)(2,1)} %slice.26), channel_id=1, source_target_pairs={{0,32},{1,33},{2,34},{3,35},{4,36},{5,37},{6,38},{7,39},{8,40},{9,... | collective-permute-start | bytes 1572872 | tf_op jit(solution)/shard_map/ppermute | solution.py:36
  73.3 26.4 %collective-permute-start.4 = (bf16[128,2048]{1,0:T(8,128)(2,1)}, bf16[128,2048]{1,0:T(8,128)(2,1)}, u32[]{:S(2)}, u32[]{:S(2)}) collective-permute-start(bf16[128,2048]{1,0:T(8,128)(2,1)} %slice.27), channel_id=1, source_target_pairs={{0,96},{1,97},{2,98},{3,99},{4,100},{5,101},{6,102},{7,103},{8,104... | collective-permute-start | bytes 1572872 | tf_op jit(solution)/shard_map/ppermute | solution.py:36
  91.8 116.6 %all-to-all-start = ((s16[16,32,2176]{2,1,0:T(8,128)(2,1)}), s16[16,32,2176]{2,1,0:T(8,128)(2,1)S(1)}, u32[]{:S(2)}, u32[]{:S(2)}) async-start(s16[16,32,2176]{2,1,0:T(8,128)(2,1)} %bitcast.32), calls=%async_computation | async-start | bytes 4456448 | tf_op jit(solution)/shard_map/all_to_all | solution.py:244
  111.8 27.6 %collective-permute-start.6 = (s16[128,2176]{1,0:T(8,128)(2,1)}, s16[128,2176]{1,0:T(8,128)(2,1)}, u32[]{:S(2)}, u32[]{:S(2)}) collective-permute-start(s16[128,2176]{1,0:T(8,128)(2,1)} %get-tuple-element.30), channel_id=1, source_target_pairs={{0,1},{1,2},{2,3},{3,0},{4,5},{5,6},{6,7},{7,4},{8,9},{9,10},{10,1... | collective-permute-start | bytes 1671176 | tf_op jit(solution)/shard_map/ppermute | solution.py:36
  113.2 37.4 %collective-permute-start.7 = (s16[128,2176]{1,0:T(8,128)(2,1)}, s16[128,2176]{1,0:T(8,128)(2,1)S(1)}, u32[]{:S(2)}, u32[]{:S(2)}) collective-permute-start(s16[128,2176]{1,0:T(8,128)(2,1)} %copy-done.16), channel_id=1, source_target_pairs={{0,2},{1,3},{2,0},{3,1},{4,6},{5,7},{6,4},{7,5},{8,10},{9,11},{10,... | collective-permute-start | bytes 1671176 | tf_op jit(solution)/shard_map/ppermute | solution.py:36
  115.6 37.0 %collective-permute-start.8 = (s16[128,2176]{1,0:T(8,128)(2,1)}, s16[128,2176]{1,0:T(8,128)(2,1)S(1)}, u32[]{:S(2)}, u32[]{:S(2)}) collective-permute-start(s16[128,2176]{1,0:T(8,128)(2,1)} %copy-done.15), channel_id=1, source_target_pairs={{0,3},{1,0},{2,1},{3,2},{4,7},{5,4},{6,5},{7,6},{8,11},{9,8},{10,9... | collective-permute-start | bytes 1671176 | tf_op jit(solution)/shard_map/ppermute | solution.py:36
  126.5 36.7 %collective-permute-start.16 = (s16[128,2176]{1,0:T(8,128)(2,1)S(1)}, s16[128,2176]{1,0:T(8,128)(2,1)S(1)}, u32[]{:S(2)}, u32[]{:S(2)}) collective-permute-start(s16[128,2176]{1,0:T(8,128)(2,1)S(1)} %get-tuple-element.38), channel_id=1, source_target_pairs={{0,1},{1,2},{2,3},{3,0},{4,5},{5,6},{6,7},{7,4},{8,9},{9,10},{10,1... | collective-permute-start | bytes 1671176 | tf_op jit(solution)/shard_map/ppermute | solution.py:36
  127.1 47.4 %collective-permute-start.17 = (s16[128,2176]{1,0:T(8,128)(2,1)S(1)}, s16[128,2176]{1,0:T(8,128)(2,1)S(1)}, u32[]{:S(2)}, u32[]{:S(2)}) collective-permute-start(s16[128,2176]{1,0:T(8,128)(2,1)S(1)} %get-tuple-element.39), channel_id=1, source_target_pairs={{0,2},{1,3},{2,0},{3,1},{4,6},{5,7},{6,4},{7,5},{8,10},{9,11},{10,... | collective-permute-start | bytes 1671176 | tf_op jit(solution)/shard_map/ppermute | solution.py:36
  139.5 37.3 %collective-permute-start.18 = (s16[128,2176]{1,0:T(8,128)(2,1)S(1)}, s16[128,2176]{1,0:T(8,128)(2,1)S(1)}, u32[]{:S(2)}, u32[]{:S(2)}) collective-permute-start(s16[128,2176]{1,0:T(8,128)(2,1)S(1)} %get-tuple-element.40), channel_id=1, source_target_pairs={{0,3},{1,0},{2,1},{3,2},{4,7},{5,4},{6,5},{7,6},{8,11},{9,8},{10,9... | collective-permute-start | bytes 1671176 | tf_op jit(solution)/shard_map/ppermute | solution.py:36
  150.5 30.7 %collective-permute-start.22 = (s16[128,2176]{1,0:T(8,128)(2,1)S(1)}, s16[128,2176]{1,0:T(8,128)(2,1)S(1)}, u32[]{:S(2)}, u32[]{:S(2)}) collective-permute-start(s16[128,2176]{1,0:T(8,128)(2,1)S(1)} %get-tuple-element.46), channel_id=1, source_target_pairs={{0,4},{1,5},{2,6},{3,7},{4,16},{5,17},{6,18},{7,19},{8,12},{9,13},... | collective-permute-start | bytes 1671176 | tf_op jit(solution)/shard_map/ppermute | solution.py:36
  152.6 28.7 %collective-permute-start.23 = (s16[128,2176]{1,0:T(8,128)(2,1)S(1)}, s16[128,2176]{1,0:T(8,128)(2,1)S(1)}, u32[]{:S(2)}, u32[]{:S(2)}) collective-permute-start(s16[128,2176]{1,0:T(8,128)(2,1)S(1)} %get-tuple-element.47), channel_id=1, source_target_pairs={{0,16},{1,17},{2,18},{3,19},{4,20},{5,21},{6,22},{7,23},{8,24},{9,... | collective-permute-start | bytes 1671176 | tf_op jit(solution)/shard_map/ppermute | solution.py:36
  163.2 19.4 %collective-permute-start.24 = (s16[128,2176]{1,0:T(8,128)(2,1)S(1)}, s16[128,2176]{1,0:T(8,128)(2,1)S(1)}, u32[]{:S(2)}, u32[]{:S(2)}) collective-permute-start(s16[128,2176]{1,0:T(8,128)(2,1)S(1)} %get-tuple-element.48), channel_id=1, source_target_pairs={{0,20},{1,21},{2,22},{3,23},{4,0},{5,1},{6,2},{7,3},{8,28},{9,29},... | collective-permute-start | bytes 1671176 | tf_op jit(solution)/shard_map/ppermute | solution.py:36
  181.2 18.0 %collective-permute-start.9 = (s16[32,2176]{1,0:T(8,128)(2,1)S(1)}, s16[32,2176]{1,0:T(8,128)(2,1)S(1)}, u32[]{:S(2)}, u32[]{:S(2)}) collective-permute-start(s16[32,2176]{1,0:T(8,128)(2,1)S(1)} %get-tuple-element.34), channel_id=1, source_target_pairs={{0,4},{1,5},{2,6},{3,7},{4,16},{5,17},{6,18},{7,19},{8,12},{9,13},... | collective-permute-start | bytes 417800 | tf_op jit(solution)/shard_map/ppermute | solution.py:36
  181.3 18.6 %collective-permute-start.19 = (s16[32,2176]{1,0:T(8,128)(2,1)S(1)}, s16[32,2176]{1,0:T(8,128)(2,1)S(1)}, u32[]{:S(2)}, u32[]{:S(2)}) collective-permute-start(s16[32,2176]{1,0:T(8,128)(2,1)S(1)} %get-tuple-element.42), channel_id=1, source_target_pairs={{0,4},{1,5},{2,6},{3,7},{4,16},{5,17},{6,18},{7,19},{8,12},{9,13},... | collective-permute-start | bytes 417800 | tf_op jit(solution)/shard_map/ppermute | solution.py:36
  182.6 22.4 %collective-permute-start.20 = (s16[32,2176]{1,0:T(8,128)(2,1)}, s16[32,2176]{1,0:T(8,128)(2,1)}, u32[]{:S(2)}, u32[]{:S(2)}) collective-permute-start(s16[32,2176]{1,0:T(8,128)(2,1)} %get-tuple-element.43), channel_id=1, source_target_pairs={{0,16},{1,17},{2,18},{3,19},{4,20},{5,21},{6,22},{7,23},{8,24},{9,... | collective-permute-start | bytes 417800 | tf_op jit(solution)/shard_map/ppermute | solution.py:36
  187.8 17.2 %collective-permute-start.21 = (s16[32,2176]{1,0:T(8,128)(2,1)}, s16[32,2176]{1,0:T(8,128)(2,1)}, u32[]{:S(2)}, u32[]{:S(2)}) collective-permute-start(s16[32,2176]{1,0:T(8,128)(2,1)} %get-tuple-element.44), channel_id=1, source_target_pairs={{0,20},{1,21},{2,22},{3,23},{4,0},{5,1},{6,2},{7,3},{8,28},{9,29},... | collective-permute-start | bytes 417800 | tf_op jit(solution)/shard_map/ppermute | solution.py:36
  191.2 15.9 %collective-permute-start.25 = (s16[32,2176]{1,0:T(8,128)(2,1)}, s16[32,2176]{1,0:T(8,128)(2,1)}, u32[]{:S(2)}, u32[]{:S(2)}) collective-permute-start(s16[32,2176]{1,0:T(8,128)(2,1)} %get-tuple-element.50), channel_id=1, source_target_pairs={{0,1},{1,2},{2,3},{3,0},{4,5},{5,6},{6,7},{7,4},{8,9},{9,10},{10,1... | collective-permute-start | bytes 417800 | tf_op jit(solution)/shard_map/ppermute | solution.py:36
  (27 other events, 201.7 us)

commit v2 on v0

v2 whole, which is shorter than its diff:
```python
import functools
import jax
import jax.numpy as jnp
from jax import lax
from jax.experimental import pallas as pl
from jax.experimental.pallas import tpu as pltpu
from jax.sharding import PartitionSpec as P

AXES = ("oi", "oj", "vert")
SIDE = 4
LANES = 128
LANE_TILE = 512
TOP = 32512.0
STEPS_PER_OCTAVE = 64.0
VMEM_BYTES = 16 * 1024 * 1024


def place_of(i):
    x, rest = divmod(i, 32)
    y_hi, rest = divmod(rest, 16)
    core, rest = divmod(rest, 8)
    y_lo, z = divmod(rest, 4)
    return x, 2 * y_hi + y_lo, z, core


def index_in_plane(y, z, core):
    y, z = y % SIDE, z % SIDE
    return (((y // 2) * 2 + core) * 2 + y % 2) * 4 + z


def shift(value, dx=0, dcore=0, dplane=None):
    pairs = []
    for i in range(128):
        x, y, z, core = place_of(i)
        dy, dz = dplane[core] if dplane else (0, 0)
        pairs.append((i, (x + dx) % SIDE * 32 + index_in_plane(y + dy, z + dz, (core + dcore) % 2)))
    return lax.ppermute(value, AXES, pairs)


def after(value, *others):
    return lax.optimization_barrier((value, others))[0]


def lane_index(rows):
    return lax.broadcasted_iota(jnp.int32, (rows, LANES), 1)


def encode(values, steps, heads, tile):
    for at in range(0, values.shape[0], 32):
        rows = pl.ds(at, min(32, values.shape[0] - at))
        part = values[rows, :]
        peak = jnp.maximum(jnp.max(jnp.abs(part), axis=1, keepdims=True), 1e-30)
        code = jnp.ceil(jnp.log2(peak) * STEPS_PER_OCTAVE)
        scaled = jnp.round(part * (jnp.exp2(code * (-1.0 / STEPS_PER_OCTAVE)) * TOP))
        steps[rows, :] = scaled.astype(jnp.int32).astype(jnp.int16)
        heads[rows, :] = jnp.where(lane_index(rows.size) == tile, code.astype(jnp.int32), heads[rows, :])


def load_codes(ref, rows, tile):
    heads = ref[rows, pl.ds(ref.shape[1] - LANES, LANES)].astype(jnp.int32)
    code = jnp.sum(jnp.where(lane_index(heads.shape[0]) == tile, heads, 0), axis=1, keepdims=True)
    scale = jnp.exp2(code.astype(jnp.float32) * (1.0 / STEPS_PER_OCTAVE)) * (1.0 / TOP)
    return ref[rows, pl.ds(tile * LANE_TILE, LANE_TILE)].astype(jnp.int32).astype(jnp.float32) * scale


def params():
    return pltpu.CompilerParams(vmem_limit_bytes=VMEM_BYTES)


def cost(micros):
    return pl.CostEstimate(flops=int(micros * 1.15e9), bytes_accessed=1000, transcendentals=0)


def turned_kernel(core, live, values, mine, theirs, scratch):
    tile = pl.program_id(0)
    for k in range(values.shape[0] // LANES):
        part = values[pl.ds(k * LANES, LANES), :]
        kept = jnp.where(live[k, tile] != 0, part, jnp.zeros_like(part))
        scratch[:, pl.ds(k * LANES, LANES)] = kept.T
    mine[0] = scratch[pl.ds(pl.multiple_of(core[0] * 64, 16), 64), :]
    theirs[0] = scratch[pl.ds(pl.multiple_of((1 - core[0]) * 64, 16), 64), :]


def turned(core, values, live):
    depth, columns = values.shape
    half = jax.ShapeDtypeStruct((columns // LANES, 64, depth), jnp.bfloat16)
    smem = pl.BlockSpec(memory_space=pltpu.SMEM)
    return pl.pallas_call(
        turned_kernel,
        grid=(columns // LANES,),
        out_shape=[half, half],
        in_specs=[smem, smem, pl.BlockSpec((depth, LANES), lambda t: (0, t))],
        out_specs=[pl.BlockSpec((1, 64, depth), lambda t: (t, 0, 0))] * 2,
        scratch_shapes=[pltpu.VMEM((LANES, depth), jnp.bfloat16)],
        compiler_params=params(),
        cost_estimate=cost(2.5),
    )(core.reshape(1), live, values)


def amps_kernel(live, values, out):
    tile = pl.program_id(0)
    for r in range(values.shape[0] // LANES):
        for k in range(values.shape[1] // LANES):
            part = values[pl.ds(r * LANES, LANES), pl.ds(k * LANES, LANES)]
            kept = jnp.where(live[tile * (values.shape[0] // LANES) + r, k] != 0, part, jnp.zeros_like(part))
            out[pl.ds(k * LANES, LANES), pl.ds(r * LANES, LANES)] = kept.T


def turned_amps(values, live):
    rows, depth = values.shape
    return pl.pallas_call(
        amps_kernel,
        grid=(rows // LANE_TILE,),
        out_shape=jax.ShapeDtypeStruct((depth, rows), jnp.bfloat16),
        in_specs=[pl.BlockSpec(memory_space=pltpu.SMEM), pl.BlockSpec((LANE_TILE, depth), lambda t: (t, 0))],
        out_specs=pl.BlockSpec((depth, LANE_TILE), lambda t: (0, t)),
        compiler_params=params(),
        cost_estimate=cost(4),
    )(live, values)


def product_kernel(direct, sizes, places, n_arrays, table, *refs):
    arrays, (a_own, a_other, *outs, acc, steps, heads) = refs[:n_arrays], refs[n_arrays:]
    heads[...] = jnp.zeros_like(heads)
    blocks = [n for n in sizes for _ in range(2)]
    runs = []
    for to in range(16 if direct else 4):
        row, base = to * sum(sizes) if direct else 0, 0
        for part, n in enumerate(sizes):
            for q in range(1 if direct else 4):
                at = table[part * 16 + to] if direct else table[part * 16 + to * 4 + q]
                runs.append((0 if direct else to, row, n, pl.ds(pl.multiple_of(base + at * n, 16), n)))
                row += n
            base += 16 * n

    def one_tile(tile, carry):
        lanes = pl.ds(pl.multiple_of(tile * LANE_TILE, LANE_TILE), LANE_TILE)
        base = 0
        for n, ((i, own), (k, other)) in zip(blocks, places, strict=True):
            acc[pl.ds(base, 8 * n), :] = jnp.dot(
                arrays[i][pl.ds(own, 8 * n), :], a_own[:, lanes], preferred_element_type=jnp.float32
            ) + jnp.dot(arrays[k][pl.ds(other, 8 * n), :], a_other[:, lanes], preferred_element_type=jnp.float32)
            base += 8 * n

        encode(acc, steps, heads, tile)
        for to, row, n, source in runs:
            if to == 0 and not direct:
                outs[0][pl.ds(row, n), lanes] = acc[source, :]
            else:
                outs[to][pl.ds(row, n), lanes] = steps[source, :]
        return carry

    lax.fori_loop(0, a_own.shape[1] // LANE_TILE, one_tile, 0)
    for to, row, n, source in runs:
        if direct or to > 0:
            outs[to][pl.ds(row, n), pl.ds(a_own.shape[1], LANES)] = heads[source, :].astype(jnp.int16)


def products(direct, sizes, table, operands, a_own, a_other):
    rows, total = a_own.shape[1], sum(sizes)
    if direct:
        out_shape = [jax.ShapeDtypeStruct((16 * total, rows + LANES), jnp.int16)]
    else:
        out_shape = [jax.ShapeDtypeStruct((4 * total, rows), jnp.float32)] + [
            jax.ShapeDtypeStruct((4 * total, rows + LANES), jnp.int16)
        ] * 3
    arrays = []
    for array, _ in operands:
        if not any(array is known for known in arrays):
            arrays.append(array)
    where = [(next(i for i, known in enumerate(arrays) if known is array), row) for array, row in operands]
    vmem = pl.BlockSpec(memory_space=pltpu.VMEM)
    return pl.pallas_call(
        functools.partial(product_kernel, direct, sizes, list(zip(where[::2], where[1::2])), len(arrays)),
        out_shape=out_shape,
        in_specs=[pl.BlockSpec(memory_space=pltpu.SMEM)] + [vmem] * (len(arrays) + 2),
        out_specs=[vmem] * len(out_shape),
        scratch_shapes=[
            pltpu.VMEM((16 * total, LANE_TILE), jnp.float32),
            pltpu.VMEM((16 * total, LANE_TILE), jnp.int16),
            pltpu.VMEM((16 * total, LANES), jnp.int32),
        ],
        compiler_params=params(),
        cost_estimate=cost(1.5 + total / 5),
    )(table, *arrays, a_own, a_other)


def join_kernel(sizes, table, kept, one, two, three, *outs_and_scratch):
    *outs, total, steps, heads = outs_and_scratch
    heads[...] = jnp.zeros_like(heads)
    everything = pl.ds(0, kept.shape[0])
    runs = []
    for to in range(4):
        row = base = 0
        for part, n in enumerate(sizes):
            runs.append((to, row, n, pl.ds(pl.multiple_of(base + table[part * 4 + to] * n, 16), n)))
            row, base = row + n, base + 4 * n
    for tile in range(kept.shape[1] // LANE_TILE):
        lanes = pl.ds(tile * LANE_TILE, LANE_TILE)
        total[...] = kept[:, lanes] + sum(load_codes(ref, everything, tile) for ref in (one, two, three))
        encode(total, steps, heads, tile)
        for to, row, n, source in runs:
            outs[to][pl.ds(row, n), lanes] = steps[source, :] if to else total[source, :]
    for to, row, n, source in runs:
        if to:
            outs[to][pl.ds(row, n), pl.ds(kept.shape[1], LANES)] = heads[source, :].astype(jnp.int16)


def join(sizes, table, kept, arrived):
    rows, total = kept.shape[1], sum(sizes)
    out_shape = [jax.ShapeDtypeStruct((total, rows), jnp.float32)] + [
        jax.ShapeDtypeStruct((total, rows + LANES), jnp.int16)
    ] * 3
    vmem = pl.BlockSpec(memory_space=pltpu.VMEM)
    return pl.pallas_call(
        functools.partial(join_kernel, sizes),
        out_shape=out_shape,
        in_specs=[pl.BlockSpec(memory_space=pltpu.SMEM)] + [vmem] * 4,
        out_specs=[vmem] * 4,
        scratch_shapes=[
            pltpu.VMEM((4 * total, LANE_TILE), jnp.float32),
            pltpu.VMEM((4 * total, LANE_TILE), jnp.int16),
            pltpu.VMEM((4 * total, LANES), jnp.int32),
        ],
        compiler_params=params(),
        cost_estimate=cost(2.3),
    )(table, kept, *arrived)


def last_kernel(kept, one, two, three, out):
    everything = pl.ds(0, kept.shape[0])
    for tile in range(kept.shape[1] // LANE_TILE):
        lanes = pl.ds(tile * LANE_TILE, LANE_TILE)
        out[:, lanes] = kept[:, lanes] + sum(load_codes(ref, everything, tile) for ref in (one, two, three))


def last(kept, arrived):
    vmem = pl.BlockSpec(memory_space=pltpu.VMEM)
    return pl.pallas_call(
        last_kernel,
        out_shape=jax.ShapeDtypeStruct(kept.shape, jnp.float32),
        in_specs=[vmem] * 4,
        out_specs=vmem,
        compiler_params=params(),
        cost_estimate=cost(1),
    )(kept, *arrived)


def sum_kernel(arrived, out):
    n = out.shape[0]
    for tile in range(out.shape[1] // LANE_TILE):
        out[:, pl.ds(tile * LANE_TILE, LANE_TILE)] = sum(
            load_codes(arrived, pl.ds(k * n, n), tile) for k in range(16)
        )


def sum_of(arrived):
    total, rows = arrived.shape[0] // 16, arrived.shape[1] - LANES
    vmem = pl.BlockSpec(memory_space=pltpu.VMEM)
    return pl.pallas_call(
        sum_kernel,
        out_shape=jax.ShapeDtypeStruct((total, rows), jnp.float32),
        in_specs=[vmem],
        out_specs=vmem,
        compiler_params=params(),
        cost_estimate=cost(1),
    )(arrived)


PLANE_GROUPS = [[index_in_plane(y, z, core) for y in range(4) for z in range(4)] for core in range(2)]
CHUNKS = (32, 16, 16)
GROUPS = (
    (True, (("near", 0),)),
    (False, (("near", 1), ("far", 0))),
    (False, (("near", 2), ("far", 1))),
    (True, (("far", 2),)),
)


def per_device(amps, integrals, amp_live, int_live, row_gap, col_gap):
    x, oj, vert = (lax.axis_index(axis).astype(jnp.int32) for axis in AXES)
    core, y, z = oj % 2, (oj // 2) * 2 + vert // 4, vert % 4
    around = jnp.arange(4, dtype=jnp.int32)

    mine, theirs = turned(core, integrals, int_live)
    depth = mine.shape[2]
    starts = [sum(CHUNKS[:j]) for j in range(len(CHUNKS))]
    cut = lambda half, j: half[:, starts[j]:starts[j] + CHUNKS[j]].reshape(-1, depth)
    swapped = shift(theirs, dcore=1)
    own = [[(cut(mine, j), 0), (cut(swapped, j), 0)] for j in range(len(CHUNKS))]
    join_all = lax.optimization_barrier

    def send(forward, j):
        following = [own[j][0][0], own[j][1][0]] if j < len(CHUNKS) else []
        return (
            shift(jnp.concatenate(forward[0] + following), dx=1),
            shift(jnp.concatenate(forward[1] + following), dx=-1),
        )

    left, right, far = [], [], []

    def receive(arrived, j):
        skip = 8 * CHUNKS[j - 1] if j else 0
        if j:
            far.append([(arrived[0], 0), (arrived[1], 0)])
        if j < len(CHUNKS):
            for side, array in zip((left, right), arrived):
                side.append([(array, skip), (array, skip + 8 * CHUNKS[j])])

    def forward(j):
        held = lambda spot: lax.slice_in_dim(spot[0], spot[1], spot[1] + 8 * CHUNKS[j])
        return [held(left[j][0])], [held(right[j][1])]

    first = send(([], []), 0)
    a_own = turned_amps(amps, after(amp_live, mine))
    a_other = shift(a_own, dcore=1)
    *first, a_own, a_other = join_all((*first, a_own, a_other))
    receive(first, 0)

    def y_run(first_block, places):
        pair = jnp.where(places // 2 == (first_block % 4) // 2, 0, 1)
        return pair * 2 + places % 2

    def spread(direct, parts, previous):
        sizes = tuple(CHUNKS[j] for _, j in parts)
        operands, tables, later = [], [], []
        for kind, j in parts:
            first = x - 1 if kind == "near" else x
            operands += left[j] + right[j] if kind == "near" else own[j] + far[j]
            if direct:
                tables.append((y_run(first, around)[:, None] * 4 + around[None, :]).reshape(16))
            else:
                z_to, y_to = (z + around) % 4, y_run(first, (y + around) % 4)
                z_first = around[None, :] * 4 + z_to[:, None]
                y_first = y_to[:, None] * 4 + around[None, :]
                tables.append(jnp.where(core == 0, z_first, y_first).reshape(16))
                later.append(jnp.where(core == 0, y_to, z_to))
        table = after(jnp.concatenate(tables).astype(jnp.int32), *previous)
        if direct:
            (sent,) = products(True, sizes, table, operands, a_own, a_other)
            got = lax.all_to_all(sent, ("oj", "vert"), 0, 0, axis_index_groups=PLANE_GROUPS, tiled=True)
            return sum_of(got), [sent]
        kept, *sent = products(False, sizes, table, operands, a_own, a_other)
        at_once = sent
        arrived = [shift(s, dplane=((0, d + 1), (d + 1, 0))) for d, s in enumerate(sent)]
        kept, *sent = join(sizes, jnp.concatenate(later).astype(jnp.int32), kept, arrived)
        return last(kept, [shift(s, dplane=((d + 1, 0), (0, d + 1))) for d, s in enumerate(sent)]), at_once

    found, previous = {}, []
    for j, (direct, parts) in enumerate(GROUPS):
        if j < len(CHUNKS):
            coming = send(forward(j), j + 1)
        result, previous = spread(direct, parts, previous)
        if j < len(CHUNKS):
            *coming, previous = join_all((*coming, previous))
            receive(coming, j + 1)
        row = 0
        for kind, j in parts:
            found[kind, j] = result[row:row + CHUNKS[j]]
            row += CHUNKS[j]
    near, far = (jnp.concatenate([found[kind, j] for j in range(len(CHUNKS))]) for kind in ("near", "far"))
    far_is_mine = core == x % 2
    kept = jnp.where(far_is_mine, far, near)
    swapped = shift(jnp.where(far_is_mine, near, far), dcore=1)
    resid = jnp.where(core == 0, jnp.concatenate([kept, swapped]), jnp.concatenate([swapped, kept])).T
    return resid / (row_gap[:, None] + col_gap[None, :])


def solution(mesh):
    return jax.shard_map(
        per_device,
        mesh=mesh,
        in_specs=(
            P("oi", ("oj", "vert")),
            P(("oj", "vert"), "oi"),
            P("oi", ("oj", "vert")),
            P(("oj", "vert"), "oi"),
            P("oi"),
            P(("oj", "vert")),
        ),
        out_specs=P("oi", ("oj", "vert")),
        check_vma=False,
    )
```

time: 497 us -> 168 us (0.34)
  waiting for transfers between devices: 450 us -> 45.1 us
  Pallas kernels: 0 us -> 55.4 us
  starting transfers between devices: 0.04 us -> 41.3 us
  matrix products: 25.5 us -> 0 us
  local copies, waits for them, and re-layouts: 2.35 us -> 20.3 us
  between operations: 13.4 us -> 0.4 us
    reduce_scatter x1 -> x0, waiting for transfers between devices: 364 us -> none  [per_device(): lax.psum_scatter(lax.dot_general(int_whole, amp_tiles, (((0,), (1,)), (()...]
    all_gather x1 -> x0, waiting for transfers between devices: 86.3 us -> none  [per_device(): int_whole = lax.all_gather(int_tiles, 'oi', axis=1, tiled=True)]
    pallas_call x0 -> x12, Pallas kernels: none -> 55.4 us  [the longest x4 41.7 us: products(): pl.pallas_call(functools.partial(product_kernel, direct, sizes, list(zip(...]
    ppermute x0 -> x23, waiting for transfers between devices: none -> 45.1 us  [shift(): return lax.ppermute(value, AXES, pairs)]
    ppermute x0 -> x23, starting transfers between devices: none -> 25.9 us  [shift(): return lax.ppermute(value, AXES, pairs)]
    dot_general x1 -> x0, matrix products: 25.5 us -> none  [per_device(): lax.dot_general(int_whole, amp_tiles, (((0,), (1,)), ((), ())), preferred...]
    all_to_all x0 -> x2, starting transfers between devices: none -> 15.4 us  [spread(): lax.all_to_all(sent, ('oj', 'vert'), 0, 0, axis_index_groups=PLANE_GROUPS...]
    unnamed x6 -> x40, local copies, waits for them, and re-layouts: 0.01 us -> 11.4 us
  transfers between devices with their start and end apart: 2 -> 25, of which waited for: 2 -> 9; matrix products, arithmetic and copies ran while one was open for 0% -> 5% of each run, Pallas kernels for 0% -> 29%
where the time goes in v2:
time: 168 us; the launch traced here: 167 us
  Pallas kernels  55.4 us (33%)
  waiting for transfers between devices  45.1 us (27%)
  starting transfers between devices  41.3 us (25%)
  local copies, waits for them, and re-layouts  20.3 us (12%)
  other arithmetic  4.55 us (3%)
    ppermute x23, waiting for transfers between devices, shift(): return lax.ppermute(value, AXES, pairs)  45.1 us
    pallas_call x4, Pallas kernels, products(): pl.pallas_call(functools.partial(product_kernel, direct, sizes, list(zip(...  41.7 us
    ppermute x23, starting transfers between devices, shift(): return lax.ppermute(value, AXES, pairs)  25.9 us
    all_to_all x2, starting transfers between devices, spread(): lax.all_to_all(sent, ('oj', 'vert'), 0, 0, axis_index_groups=PLANE_GROUPS...  15.4 us
    unnamed x40, local copies, waits for them, and re-layouts  11.4 us
    pallas_call x2, Pallas kernels, join(): pl.pallas_call(functools.partial(join_kernel, sizes), out_shape=out_shape...  5.46 us
    pallas_call x1, Pallas kernels, turned_amps(): pl.pallas_call(amps_kernel, grid=(rows // LANE_TILE,), out_shape=jax.Shap...  3.78 us
    slice x4, local copies, waits for them, and re-layouts, per_device(): half[:, starts[j]:starts[j] + CHUNKS[j]].reshape(-1, depth)  3.65 us
  transfers between devices with their start and end apart: 25, of which 9 were waited for; matrix products, arithmetic and copies ran while one was open for 5% of the time, Pallas kernels for 29%

profile of v2, /device:TPU:1, one launch (start us, length us, event | category | flops | bytes accessed | tf_op | source)
XLA Modules:
  0.0 167.0 jit_solution(7367622225699974745)
XLA Ops:
  0.0 1.6 copy-done.9
  2.3 2.4 %shard_map.64 = (bf16[8,64,1024]{2,1,0:T(8,128)(2,1)S(1)}, bf16[8,64,1024]{2,1,0:T(8,128)(2,1)S(1)}) custom-call(s32[1]{0:T(128)} %bitcast.core, s32[8,8]{1,0:T(8,128)S(1)} %copy-done.12, bf16[1024,1024]{1,0:T(8,128)(2,1)S(1)} %copy-done.9), custom_call_target="tpu_custom_call" | custom-call | flops 2875000064 | bytes 1000 | tf_op jit(solution)/shard_map/pallas_call | solution.py:88
  4.8 2.2 %copy-done.8 = bf16[2048,1024]{1,0:T(8,128)(2,1)S(1)} copy-done((bf16[2048,1024]{1,0:T(8,128)(2,1)S(1)}, bf16[2048,1024]{1,0:T(8,128)(2,1)}, u32[]{:S(2)}) %copy-start.8) | copy-done | bytes 4194328
  7.0 3.8 %shard_map.65.refs_2_.refs_4_ = bf16[1024,2048]{1,0:T(8,128)(2,1)} custom-call(s32[16,8]{1,0:T(8,128)S(1)} %copy.7.live, bf16[2048,1024]{1,0:T(8,128)(2,1)S(1)} %copy-done.8), custom_call_target="tpu_custom_call" | custom-call | flops 4600000000 | bytes 1000 | tf_op jit(solution)/shard_map/pallas_call | solution.py:111
  12.4 8.0 %collective-permute-done = bf16[8,64,1024]{2,1,0:T(8,128)(2,1)} collective-permute-done((bf16[8,64,1024]{2,1,0:T(8,128)(2,1)S(1)}, bf16[8,64,1024]{2,1,0:T(8,128)(2,1)}, u32[]{:S(2)}, u32[]{:S(2)}) %collective-permute-start) | collective-permute-done | bytes 1048608 | tf_op jit(solution)/shard_map/ppermute | solution.py:37
  22.6 2.6 %collective-permute-start.2 = (bf16[512,1024]{1,0:T(8,128)(2,1)}, bf16[512,1024]{1,0:T(8,128)(2,1)S(1)}, u32[]{:S(2)}, u32[]{:S(2)}) collective-permute-start(bf16[512,1024]{1,0:T(8,128)(2,1)} %pad_maximum_fusion.4), channel_id=1, source_target_pairs={{0,96},{1,97},{2,98},{3,99},{4,100},{5,101},{6,102},{7,103},{8,104... | collective-permute-start | bytes 3145736 | tf_op jit(solution)/shard_map/ppermute | solution.py:37
  26.5 1.8 %fusion.17 = (bf16[8,16,1024]{2,1,0:T(8,128)(2,1)S(1)}, bf16[8,16,1024]{2,1,0:T(8,128)(2,1)}) fusion(bf16[8,64,1024]{2,1,0:T(8,128)(2,1)} %collective-permute-done), kind=kLoop, calls=%fused_computation.60 | loop fusion | bytes 1048576 | tf_op jit(solution)/shard_map/slice | solution.py:288
  28.3 19.6 %collective-permute-done.2.refs_1_ = bf16[512,1024]{1,0:T(8,128)(2,1)S(1)} collective-permute-done((bf16[512,1024]{1,0:T(8,128)(2,1)}, bf16[512,1024]{1,0:T(8,128)(2,1)S(1)}, u32[]{:S(2)}, u32[]{:S(2)}) %collective-permute-start.2) | collective-permute-done | bytes 1048608 | tf_op jit(solution)/shard_map/ppermute | solution.py:37
  47.9 3.1 %collective-permute-done.1.refs_0_ = bf16[512,1024]{1,0:T(8,128)(2,1)} collective-permute-done((bf16[512,1024]{1,0:T(8,128)(2,1)}, bf16[512,1024]{1,0:T(8,128)(2,1)}, u32[]{:S(2)}, u32[]{:S(2)}) %collective-permute-start.1) | collective-permute-done | bytes 1048608 | tf_op jit(solution)/shard_map/ppermute | solution.py:37
  55.3 9.6 %shard_map.66 = s16[512,2176]{1,0:T(8,128)(2,1)S(1)} custom-call(s32[16]{0:T(128)S(1)} %add.331.table, bf16[512,1024]{1,0:T(8,128)(2,1)} %collective-permute-done.1.refs_0_, bf16[512,1024]{1,0:T(8,128)(2,1)S(1)} %collective-permute-done.2.refs_1_, bf16[1024,2048]{1,0:T(8,128)(2,1)} %shard_map.65.refs_2_.refs_4_, ...), custom_call_target="tpu_custom_call" | custom-call | flops 9084999680 | bytes 1000 | tf_op jit(solution)/shard_map/pallas_call | solution.py:173
  66.2 7.8 %all-to-all-start.1 = ((s16[16,32,2176]{2,1,0:T(8,128)(2,1)}), s16[16,32,2176]{2,1,0:T(8,128)(2,1)S(1)}, u32[]{:S(2)}, u32[]{:S(2)}) async-start(s16[16,32,2176]{2,1,0:T(8,128)(2,1)} %bitcast.16), calls=%async_computation.1 | async-start | bytes 4456448 | tf_op jit(solution)/shard_map/all_to_all | solution.py:341
  74.0 3.4 %collective-permute-done.5.refs_1_ = bf16[512,1024]{1,0:T(8,128)(2,1)} collective-permute-done((bf16[512,1024]{1,0:T(8,128)(2,1)}, bf16[512,1024]{1,0:T(8,128)(2,1)}, u32[]{:S(2)}, u32[]{:S(2)}) %collective-permute-start.5) | collective-permute-done | bytes 1048608 | tf_op jit(solution)/shard_map/ppermute | solution.py:37
  83.5 13.5 %shard_map.67 = (f32[192,2048]{1,0:T(8,128)S(1)}, s16[192,2176]{1,0:T(8,128)(2,1)S(1)}, s16[192,2176]{1,0:T(8,128)(2,1)}, s16[192,2176]{1,0:T(8,128)(2,1)}) custom-call(s32[32]{0:T(128)S(1)} %pad_add_fusion.1.table, bf16[512,1024]{1,0:T(8,128)(2,1)} %collective-permute-done.4.refs_0_, bf16[512,1024]{1,0:T(8,128)(2,1)} %collective-permute-done.5.refs_1_, ...), custom_call_target="tpu_custom_call" | custom-call | flops 12764999680 | bytes 1000 | tf_op jit(solution)/shard_map/pallas_call | solution.py:173
  99.6 2.6 %collective-permute-start.7 = (s16[192,2176]{1,0:T(8,128)(2,1)}, s16[192,2176]{1,0:T(8,128)(2,1)}, u32[]{:S(2)}, u32[]{:S(2)}) collective-permute-start(s16[192,2176]{1,0:T(8,128)(2,1)} %get-tuple-element.45), channel_id=1, source_target_pairs={{0,2},{1,3},{2,0},{3,1},{4,6},{5,7},{6,4},{7,5},{8,24},{9,25},{10,... | collective-permute-start | bytes 2506760 | tf_op jit(solution)/shard_map/ppermute | solution.py:37
  104.9 10.6 %shard_map.70 = (f32[128,2048]{1,0:T(8,128)S(1)}, s16[128,2176]{1,0:T(8,128)(2,1)}, s16[128,2176]{1,0:T(8,128)(2,1)}, s16[128,2176]{1,0:T(8,128)(2,1)}) custom-call(s32[32]{0:T(128)S(1)} %pad_add_fusion.1.table, bf16[384,1024]{1,0:T(8,128)(2,1)S(1)} %collective-permute-done.12.refs_0_, bf16[384,1024]{1,0:T(8,128)(2,1)S(1)} %collective-permute-done.13.refs_1_, ...), custom_call_target="tpu_custom_call" | custom-call | flops 9084999680 | bytes 1000 | tf_op jit(solution)/shard_map/pallas_call | solution.py:173
  117.7 1.7 %collective-permute-start.16 = (s16[128,2176]{1,0:T(8,128)(2,1)}, s16[128,2176]{1,0:T(8,128)(2,1)}, u32[]{:S(2)}, u32[]{:S(2)}) collective-permute-start(s16[128,2176]{1,0:T(8,128)(2,1)} %get-tuple-element.56), channel_id=1, source_target_pairs={{0,3},{1,0},{2,1},{3,2},{4,7},{5,4},{6,5},{7,6},{8,28},{9,29},{10,... | collective-permute-start | bytes 1671176 | tf_op jit(solution)/shard_map/ppermute | solution.py:37
  119.4 8.0 %shard_map.73 = s16[256,2176]{1,0:T(8,128)(2,1)} custom-call(s32[16]{0:T(128)S(1)} %add.336.table, bf16[128,1024]{1,0:T(8,128)(2,1)S(1)} %bitcast.27, bf16[128,1024]{1,0:T(8,128)(2,1)S(1)} %bitcast.29, bf16[128,1024]{1,0:T(8,128)(2,1)S(1)} %collective-permute-done.20.refs_2_, bf16[128,1024]{1,0:T(8,128)(2,1)S(1)} %collective-permute-done.21.refs_3_, ...), custom_call_target="tpu_custom_call" | custom-call | flops 5405000192 | bytes 1000 | tf_op jit(solution)/shard_map/pallas_call | solution.py:173
  127.4 7.6 %all-to-all-start = ((s16[16,16,2176]{2,1,0:T(8,128)(2,1)}), s16[16,16,2176]{2,1,0:T(8,128)(2,1)S(1)}, u32[]{:S(2)}, u32[]{:S(2)}) async-start(s16[16,16,2176]{2,1,0:T(8,128)(2,1)} %bitcast.7), calls=%async_computation | async-start | bytes 2228224 | tf_op jit(solution)/shard_map/all_to_all | solution.py:341
  137.6 3.0 %shard_map.68 = (f32[48,2048]{1,0:T(8,128)S(1)}, s16[48,2176]{1,0:T(8,128)(2,1)S(1)}, s16[48,2176]{1,0:T(8,128)(2,1)S(1)}, s16[48,2176]{1,0:T(8,128)(2,1)S(1)}) custom-call(s32[8]{0:T(128)S(1)} %pad_add_fusion.table, f32[192,2048]{1,0:T(8,128)S(1)} %copy-done.14, s16[192,2176]{1,0:T(8,128)(2,1)S(1)} %copy-done.11, ...), custom_call_target="tpu_custom_call" | custom-call | flops 2644999936 | bytes 1000 | tf_op jit(solution)/shard_map/pallas_call | solution.py:215
  142.1 2.4 %collective-permute-start.10 = (s16[48,2176]{1,0:T(8,128)(2,1)S(1)}, s16[48,2176]{1,0:T(8,128)(2,1)S(1)}, u32[]{:S(2)}, u32[]{:S(2)}) collective-permute-start(s16[48,2176]{1,0:T(8,128)(2,1)S(1)} %get-tuple-element.49), channel_id=1, source_target_pairs={{0,16},{1,17},{2,18},{3,19},{4,20},{5,21},{6,22},{7,23},{8,10},{9,... | collective-permute-start | bytes 626696 | tf_op jit(solution)/shard_map/ppermute | solution.py:37
  145.7 2.5 %shard_map.71 = (f32[32,2048]{1,0:T(8,128)S(1)}, s16[32,2176]{1,0:T(8,128)(2,1)S(1)}, s16[32,2176]{1,0:T(8,128)(2,1)S(1)}, s16[32,2176]{1,0:T(8,128)(2,1)S(1)}) custom-call(s32[8]{0:T(128)S(1)} %pad_add_fusion.table, f32[128,2048]{1,0:T(8,128)S(1)} %copy-done.16, s16[128,2176]{1,0:T(8,128)(2,1)} %collective-permute-done.14.one, ...), custom_call_target="tpu_custom_call" | custom-call | flops 2644999936 | bytes 1000 | tf_op jit(solution)/shard_map/pallas_call | solution.py:215
  149.4 5.2 %collective-permute-done.9.one = s16[48,2176]{1,0:T(8,128)(2,1)S(1)} collective-permute-done((s16[48,2176]{1,0:T(8,128)(2,1)S(1)}, s16[48,2176]{1,0:T(8,128)(2,1)S(1)}, u32[]{:S(2)}, u32[]{:S(2)}) %collective-permute-start.9) | collective-permute-done | bytes 208928 | tf_op jit(solution)/shard_map/ppermute | solution.py:37
  158.3 2.2 %collective-permute-done.18.two = s16[32,2176]{1,0:T(8,128)(2,1)S(1)} collective-permute-done((s16[32,2176]{1,0:T(8,128)(2,1)S(1)}, s16[32,2176]{1,0:T(8,128)(2,1)S(1)}, u32[]{:S(2)}, u32[]{:S(2)}) %collective-permute-start.18) | collective-permute-done | bytes 139296 | tf_op jit(solution)/shard_map/ppermute | solution.py:37
  162.0 1.9 %collective-permute-start.22 = (f32[64,2048]{1,0:T(8,128)S(1)}, f32[64,2048]{1,0:T(8,128)S(1)}, u32[]{:S(2)}, u32[]{:S(2)}) collective-permute-start(f32[64,2048]{1,0:T(8,128)S(1)} %get-tuple-element.64), channel_id=1, source_target_pairs={{0,8},{1,9},{2,10},{3,11},{4,12},{5,13},{6,14},{7,15},{8,0},{9,1},... | collective-permute-start | bytes 1572872 | tf_op jit(solution)/shard_map/ppermute | solution.py:37
  (113 shorter events, 39.5 us)
Async XLA Ops:
  10.8 40.2 %collective-permute-start.3 = (bf16[1024,2048]{1,0:T(8,128)(2,1)}, bf16[1024,2048]{1,0:T(8,128)(2,1)}, u32[]{:S(2)}, u32[]{:S(2)}) collective-permute-start(bf16[1024,2048]{1,0:T(8,128)(2,1)} %shard_map.65.refs_2_.refs_4_), channel_id=1, source_target_pairs={{0,8},{1,9},{2,10},{3,11},{4,12},{5,13},{6,14},{7,15},{8,0},{9,1},... | collective-permute-start | bytes 12582920 | tf_op jit(solution)/shard_map/ppermute | solution.py:37
  12.2 8.3 %collective-permute-start = (bf16[8,64,1024]{2,1,0:T(8,128)(2,1)S(1)}, bf16[8,64,1024]{2,1,0:T(8,128)(2,1)}, u32[]{:S(2)}, u32[]{:S(2)}) collective-permute-start(bf16[8,64,1024]{2,1,0:T(8,128)(2,1)S(1)} %get-tuple-element.35), channel_id=1, source_target_pairs={{0,8},{1,9},{2,10},{3,11},{4,12},{5,13},{6,14},{7,15},{8,0},{9,1},... | collective-permute-start | bytes 3145736 | tf_op jit(solution)/shard_map/ppermute | solution.py:37
  22.6 25.3 %collective-permute-start.2 = (bf16[512,1024]{1,0:T(8,128)(2,1)}, bf16[512,1024]{1,0:T(8,128)(2,1)S(1)}, u32[]{:S(2)}, u32[]{:S(2)}) collective-permute-start(bf16[512,1024]{1,0:T(8,128)(2,1)} %pad_maximum_fusion.4), channel_id=1, source_target_pairs={{0,96},{1,97},{2,98},{3,99},{4,100},{5,101},{6,102},{7,103},{8,104... | collective-permute-start | bytes 3145736 | tf_op jit(solution)/shard_map/ppermute | solution.py:37
  25.2 25.8 %collective-permute-start.1 = (bf16[512,1024]{1,0:T(8,128)(2,1)}, bf16[512,1024]{1,0:T(8,128)(2,1)}, u32[]{:S(2)}, u32[]{:S(2)}) collective-permute-start(bf16[512,1024]{1,0:T(8,128)(2,1)} %pad_maximum_fusion.4), channel_id=1, source_target_pairs={{0,32},{1,33},{2,34},{3,35},{4,36},{5,37},{6,38},{7,39},{8,40},{9,... | collective-permute-start | bytes 3145736 | tf_op jit(solution)/shard_map/ppermute | solution.py:37
  53.7 23.7 %collective-permute-start.5 = (bf16[512,1024]{1,0:T(8,128)(2,1)}, bf16[512,1024]{1,0:T(8,128)(2,1)}, u32[]{:S(2)}, u32[]{:S(2)}) collective-permute-start(bf16[512,1024]{1,0:T(8,128)(2,1)} %get-tuple-element.71), channel_id=1, source_target_pairs={{0,96},{1,97},{2,98},{3,99},{4,100},{5,101},{6,102},{7,103},{8,104... | collective-permute-start | bytes 3145736 | tf_op jit(solution)/shard_map/ppermute | solution.py:37
  53.9 24.9 %collective-permute-start.4 = (bf16[512,1024]{1,0:T(8,128)(2,1)}, bf16[512,1024]{1,0:T(8,128)(2,1)}, u32[]{:S(2)}, u32[]{:S(2)}) collective-permute-start(bf16[512,1024]{1,0:T(8,128)(2,1)} %get-tuple-element.72), channel_id=1, source_target_pairs={{0,32},{1,33},{2,34},{3,35},{4,36},{5,37},{6,38},{7,39},{8,40},{9,... | collective-permute-start | bytes 3145736 | tf_op jit(solution)/shard_map/ppermute | solution.py:37
  66.2 61.2 %all-to-all-start.1 = ((s16[16,32,2176]{2,1,0:T(8,128)(2,1)}), s16[16,32,2176]{2,1,0:T(8,128)(2,1)S(1)}, u32[]{:S(2)}, u32[]{:S(2)}) async-start(s16[16,32,2176]{2,1,0:T(8,128)(2,1)} %bitcast.16), calls=%async_computation.1 | async-start | bytes 4456448 | tf_op jit(solution)/shard_map/all_to_all | solution.py:341
  82.0 21.3 %collective-permute-start.13 = (bf16[384,1024]{1,0:T(8,128)(2,1)S(1)}, bf16[384,1024]{1,0:T(8,128)(2,1)S(1)}, u32[]{:S(2)}, u32[]{:S(2)}) collective-permute-start(bf16[384,1024]{1,0:T(8,128)(2,1)S(1)} %get-tuple-element.69), channel_id=1, source_target_pairs={{0,96},{1,97},{2,98},{3,99},{4,100},{5,101},{6,102},{7,103},{8,104... | collective-permute-start | bytes 2359304 | tf_op jit(solution)/shard_map/ppermute | solution.py:37
  82.3 20.9 %collective-permute-start.12 = (bf16[384,1024]{1,0:T(8,128)(2,1)S(1)}, bf16[384,1024]{1,0:T(8,128)(2,1)S(1)}, u32[]{:S(2)}, u32[]{:S(2)}) collective-permute-start(bf16[384,1024]{1,0:T(8,128)(2,1)S(1)} %get-tuple-element.70), channel_id=1, source_target_pairs={{0,32},{1,33},{2,34},{3,35},{4,36},{5,37},{6,38},{7,39},{8,40},{9,... | collective-permute-start | bytes 2359304 | tf_op jit(solution)/shard_map/ppermute | solution.py:37
  98.2 19.4 %collective-permute-start.6 = (s16[192,2176]{1,0:T(8,128)(2,1)S(1)}, s16[192,2176]{1,0:T(8,128)(2,1)S(1)}, u32[]{:S(2)}, u32[]{:S(2)}) collective-permute-start(s16[192,2176]{1,0:T(8,128)(2,1)S(1)} %get-tuple-element.44), channel_id=1, source_target_pairs={{0,1},{1,2},{2,3},{3,0},{4,5},{5,6},{6,7},{7,4},{8,12},{9,13},{10,... | collective-permute-start | bytes 2506760 | tf_op jit(solution)/shard_map/ppermute | solution.py:37
  99.6 35.5 %collective-permute-start.7 = (s16[192,2176]{1,0:T(8,128)(2,1)}, s16[192,2176]{1,0:T(8,128)(2,1)}, u32[]{:S(2)}, u32[]{:S(2)}) collective-permute-start(s16[192,2176]{1,0:T(8,128)(2,1)} %get-tuple-element.45), channel_id=1, source_target_pairs={{0,2},{1,3},{2,0},{3,1},{4,6},{5,7},{6,4},{7,5},{8,24},{9,25},{10,... | collective-permute-start | bytes 2506760 | tf_op jit(solution)/shard_map/ppermute | solution.py:37
  102.2 32.9 %collective-permute-start.8 = (s16[192,2176]{1,0:T(8,128)(2,1)}, s16[192,2176]{1,0:T(8,128)(2,1)}, u32[]{:S(2)}, u32[]{:S(2)}) collective-permute-start(s16[192,2176]{1,0:T(8,128)(2,1)} %get-tuple-element.46), channel_id=1, source_target_pairs={{0,3},{1,0},{2,1},{3,2},{4,7},{5,4},{6,5},{7,6},{8,28},{9,29},{10,... | collective-permute-start | bytes 2506760 | tf_op jit(solution)/shard_map/ppermute | solution.py:37
  103.3 13.1 %collective-permute-start.21 = (bf16[128,1024]{1,0:T(8,128)(2,1)S(1)}, bf16[128,1024]{1,0:T(8,128)(2,1)S(1)}, u32[]{:S(2)}, u32[]{:S(2)}) collective-permute-start(bf16[128,1024]{1,0:T(8,128)(2,1)S(1)} %slice.61), channel_id=1, source_target_pairs={{0,96},{1,97},{2,98},{3,99},{4,100},{5,101},{6,102},{7,103},{8,104... | collective-permute-start | bytes 786440 | tf_op jit(solution)/shard_map/ppermute | solution.py:37
  104.9 12.0 %collective-permute-start.20 = (bf16[128,1024]{1,0:T(8,128)(2,1)S(1)}, bf16[128,1024]{1,0:T(8,128)(2,1)S(1)}, u32[]{:S(2)}, u32[]{:S(2)}) collective-permute-start(bf16[128,1024]{1,0:T(8,128)(2,1)S(1)} %slice.60), channel_id=1, source_target_pairs={{0,32},{1,33},{2,34},{3,35},{4,36},{5,37},{6,38},{7,39},{8,40},{9,... | collective-permute-start | bytes 786440 | tf_op jit(solution)/shard_map/ppermute | solution.py:37
  116.5 28.0 %collective-permute-start.14 = (s16[128,2176]{1,0:T(8,128)(2,1)}, s16[128,2176]{1,0:T(8,128)(2,1)}, u32[]{:S(2)}, u32[]{:S(2)}) collective-permute-start(s16[128,2176]{1,0:T(8,128)(2,1)} %get-tuple-element.54), channel_id=1, source_target_pairs={{0,1},{1,2},{2,3},{3,0},{4,5},{5,6},{6,7},{7,4},{8,12},{9,13},{10,... | collective-permute-start | bytes 1671176 | tf_op jit(solution)/shard_map/ppermute | solution.py:37
  116.9 28.8 %collective-permute-start.15 = (s16[128,2176]{1,0:T(8,128)(2,1)}, s16[128,2176]{1,0:T(8,128)(2,1)}, u32[]{:S(2)}, u32[]{:S(2)}) collective-permute-start(s16[128,2176]{1,0:T(8,128)(2,1)} %get-tuple-element.55), channel_id=1, source_target_pairs={{0,2},{1,3},{2,0},{3,1},{4,6},{5,7},{6,4},{7,5},{8,24},{9,25},{10,... | collective-permute-start | bytes 1671176 | tf_op jit(solution)/shard_map/ppermute | solution.py:37
  117.7 28.0 %collective-permute-start.16 = (s16[128,2176]{1,0:T(8,128)(2,1)}, s16[128,2176]{1,0:T(8,128)(2,1)}, u32[]{:S(2)}, u32[]{:S(2)}) collective-permute-start(s16[128,2176]{1,0:T(8,128)(2,1)} %get-tuple-element.56), channel_id=1, source_target_pairs={{0,3},{1,0},{2,1},{3,2},{4,7},{5,4},{6,5},{7,6},{8,28},{9,29},{10,... | collective-permute-start | bytes 1671176 | tf_op jit(solution)/shard_map/ppermute | solution.py:37
  127.4 33.4 %all-to-all-start = ((s16[16,16,2176]{2,1,0:T(8,128)(2,1)}), s16[16,16,2176]{2,1,0:T(8,128)(2,1)S(1)}, u32[]{:S(2)}, u32[]{:S(2)}) async-start(s16[16,16,2176]{2,1,0:T(8,128)(2,1)} %bitcast.7), calls=%async_computation | async-start | bytes 2228224 | tf_op jit(solution)/shard_map/all_to_all | solution.py:341
  140.6 14.0 %collective-permute-start.9 = (s16[48,2176]{1,0:T(8,128)(2,1)S(1)}, s16[48,2176]{1,0:T(8,128)(2,1)S(1)}, u32[]{:S(2)}, u32[]{:S(2)}) collective-permute-start(s16[48,2176]{1,0:T(8,128)(2,1)S(1)} %get-tuple-element.48), channel_id=1, source_target_pairs={{0,4},{1,5},{2,6},{3,7},{4,16},{5,17},{6,18},{7,19},{8,9},{9,10},{... | collective-permute-start | bytes 626696 | tf_op jit(solution)/shard_map/ppermute | solution.py:37
  142.1 15.6 %collective-permute-start.10 = (s16[48,2176]{1,0:T(8,128)(2,1)S(1)}, s16[48,2176]{1,0:T(8,128)(2,1)S(1)}, u32[]{:S(2)}, u32[]{:S(2)}) collective-permute-start(s16[48,2176]{1,0:T(8,128)(2,1)S(1)} %get-tuple-element.49), channel_id=1, source_target_pairs={{0,16},{1,17},{2,18},{3,19},{4,20},{5,21},{6,22},{7,23},{8,10},{9,... | collective-permute-start | bytes 626696 | tf_op jit(solution)/shard_map/ppermute | solution.py:37
  144.5 13.2 %collective-permute-start.11 = (s16[48,2176]{1,0:T(8,128)(2,1)S(1)}, s16[48,2176]{1,0:T(8,128)(2,1)S(1)}, u32[]{:S(2)}, u32[]{:S(2)}) collective-permute-start(s16[48,2176]{1,0:T(8,128)(2,1)S(1)} %get-tuple-element.50), channel_id=1, source_target_pairs={{0,20},{1,21},{2,22},{3,23},{4,0},{5,1},{6,2},{7,3},{8,11},{9,8},{... | collective-permute-start | bytes 626696 | tf_op jit(solution)/shard_map/ppermute | solution.py:37
  148.1 10.2 %collective-permute-start.17 = (s16[32,2176]{1,0:T(8,128)(2,1)S(1)}, s16[32,2176]{1,0:T(8,128)(2,1)S(1)}, u32[]{:S(2)}, u32[]{:S(2)}) collective-permute-start(s16[32,2176]{1,0:T(8,128)(2,1)S(1)} %get-tuple-element.58), channel_id=1, source_target_pairs={{0,4},{1,5},{2,6},{3,7},{4,16},{5,17},{6,18},{7,19},{8,9},{9,10},{... | collective-permute-start | bytes 417800 | tf_op jit(solution)/shard_map/ppermute | solution.py:37
  148.5 12.1 %collective-permute-start.18 = (s16[32,2176]{1,0:T(8,128)(2,1)S(1)}, s16[32,2176]{1,0:T(8,128)(2,1)S(1)}, u32[]{:S(2)}, u32[]{:S(2)}) collective-permute-start(s16[32,2176]{1,0:T(8,128)(2,1)S(1)} %get-tuple-element.59), channel_id=1, source_target_pairs={{0,16},{1,17},{2,18},{3,19},{4,20},{5,21},{6,22},{7,23},{8,10},{9,... | collective-permute-start | bytes 417800 | tf_op jit(solution)/shard_map/ppermute | solution.py:37
  154.6 5.9 %collective-permute-start.19 = (s16[32,2176]{1,0:T(8,128)(2,1)S(1)}, s16[32,2176]{1,0:T(8,128)(2,1)S(1)}, u32[]{:S(2)}, u32[]{:S(2)}) collective-permute-start(s16[32,2176]{1,0:T(8,128)(2,1)S(1)} %get-tuple-element.60), channel_id=1, source_target_pairs={{0,20},{1,21},{2,22},{3,23},{4,0},{5,1},{6,2},{7,3},{8,11},{9,8},{... | collective-permute-start | bytes 417800 | tf_op jit(solution)/shard_map/ppermute | solution.py:37
  (23 other events, 129.0 us)

commit v3 on v2

--- a/solution.py
+++ b/solution.py
@@ -12,7 +12,7 @@
 LANE_TILE = 512
 TOP = 32512.0
 STEPS_PER_OCTAVE = 64.0
-VMEM_BYTES = 16 * 1024 * 1024
+VMEM_BYTES = 24 * 1024 * 1024
 
 
 def place_of(i):
@@ -97,92 +97,126 @@
     )(core.reshape(1), live, values)
 
 
-def amps_kernel(live, values, out):
+def masked_kernel(live_own, live_other, own, other, out_own, out_other):
     tile = pl.program_id(0)
-    for r in range(values.shape[0] // LANES):
-        for k in range(values.shape[1] // LANES):
-            part = values[pl.ds(r * LANES, LANES), pl.ds(k * LANES, LANES)]
-            kept = jnp.where(live[tile * (values.shape[0] // LANES) + r, k] != 0, part, jnp.zeros_like(part))
-            out[pl.ds(k * LANES, LANES), pl.ds(r * LANES, LANES)] = kept.T
-
-
-def turned_amps(values, live):
-    rows, depth = values.shape
-    return pl.pallas_call(
-        amps_kernel,
+    for live, values, out in ((live_own, own, out_own), (live_other, other, out_other)):
+        for r in range(values.shape[0] // LANES):
+            for k in range(values.shape[1] // LANES):
+                spot = (pl.ds(r * LANES, LANES), pl.ds(k * LANES, LANES))
+                part = values[spot]
+                kept = live[tile * (values.shape[0] // LANES) + r, k] != 0
+                out[spot] = jnp.where(kept, part, jnp.zeros_like(part))
+
+
+def masked_amps(live_own, live_other, own, other):
+    rows, depth = own.shape
+    block = pl.BlockSpec((LANE_TILE, depth), lambda t: (t, 0))
+    return pl.pallas_call(
+        masked_kernel,
         grid=(rows // LANE_TILE,),
-        out_shape=jax.ShapeDtypeStruct((depth, rows), jnp.bfloat16),
-        in_specs=[pl.BlockSpec(memory_space=pltpu.SMEM), pl.BlockSpec((LANE_TILE, depth), lambda t: (t, 0))],
-        out_specs=pl.BlockSpec((depth, LANE_TILE), lambda t: (0, t)),
-        compiler_params=params(),
-        cost_estimate=cost(4),
-    )(live, values)
-
-
-def product_kernel(direct, sizes, places, n_arrays, table, *refs):
-    arrays, (a_own, a_other, *outs, acc, steps, heads) = refs[:n_arrays], refs[n_arrays:]
+        out_shape=[pltpu.HBM(own.shape, own.dtype)] * 2,
+        in_specs=[pl.BlockSpec(memory_space=pltpu.SMEM)] * 2 + [block] * 2,
+        out_specs=[block] * 2,
+        compiler_params=params(),
+        cost_estimate=cost(6),
+    )(live_own, live_other, own, other)
+
+
+def dot_rows(a, b):
+    return lax.dot_general(a, b, (((1,), (1,)), ((), ())), preferred_element_type=jnp.float32)
+
+
+def product_kernel(mode, sizes, places, n_arrays, table, *refs):
+    direct = mode == "direct"
+    n_outs = 1 if direct else 4
+    arrays, halves, refs = refs[:n_arrays], refs[n_arrays:n_arrays + 2], refs[n_arrays + 2:]
+    outs, ready, (acc, steps, heads, amps, blocks, in_sems, out_sems) = refs[:n_outs], refs[n_outs:2 * n_outs], refs[2 * n_outs:]
+    columns, depth = halves[0].shape
+    tiles = columns // LANE_TILE
+    kept = None if direct else 0
+
+    def fetch(tile, half):
+        return pltpu.make_async_copy(
+            halves[half].at[pl.ds(tile * LANE_TILE, LANE_TILE), :], amps.at[tile, half], in_sems.at[tile, half]
+        )
+
+    def leave(out, tile):
+        lanes = pl.ds(tile * LANE_TILE, LANE_TILE if tile < tiles else LANES)
+        return pltpu.make_async_copy(ready[out].at[:, lanes], outs[out].at[:, lanes], out_sems.at[out, tile])
+
+    for half in range(2):
+        fetch(0, half).start()
+    at = 0
+    for n, spots in zip([n for n in sizes for _ in range(2)], places, strict=True):
+        for half, (i, first) in enumerate(spots):
+            blocks[half, pl.ds(at, 8 * n), :] = arrays[i][pl.ds(first, 8 * n), :]
+        at += 8 * n
     heads[...] = jnp.zeros_like(heads)
-    blocks = [n for n in sizes for _ in range(2)]
     runs = []
     for to in range(16 if direct else 4):
         row, base = to * sum(sizes) if direct else 0, 0
         for part, n in enumerate(sizes):
             for q in range(1 if direct else 4):
                 at = table[part * 16 + to] if direct else table[part * 16 + to * 4 + q]
-                runs.append((0 if direct else to, row, n, pl.ds(pl.multiple_of(base + at * n, 16), n)))
+                source = pl.ds(pl.multiple_of(base + at * n, 16), n)
+                runs.append((0 if direct else to, pl.ds(row, n), source))
                 row += n
             base += 16 * n
 
-    def one_tile(tile, carry):
-        lanes = pl.ds(pl.multiple_of(tile * LANE_TILE, LANE_TILE), LANE_TILE)
-        base = 0
-        for n, ((i, own), (k, other)) in zip(blocks, places, strict=True):
-            acc[pl.ds(base, 8 * n), :] = jnp.dot(
-                arrays[i][pl.ds(own, 8 * n), :], a_own[:, lanes], preferred_element_type=jnp.float32
-            ) + jnp.dot(arrays[k][pl.ds(other, 8 * n), :], a_other[:, lanes], preferred_element_type=jnp.float32)
-            base += 8 * n
-
+    for tile in range(tiles):
+        lanes = pl.ds(tile * LANE_TILE, LANE_TILE)
+        for half in range(2):
+            fetch(tile, half).wait()
+            if tile + 1 < tiles:
+                fetch(tile + 1, half).start()
+        acc[...] = dot_rows(blocks[0], amps[tile, 0]) + dot_rows(blocks[1], amps[tile, 1])
         encode(acc, steps, heads, tile)
-        for to, row, n, source in runs:
-            if to == 0 and not direct:
-                outs[0][pl.ds(row, n), lanes] = acc[source, :]
-            else:
-                outs[to][pl.ds(row, n), lanes] = steps[source, :]
-        return carry
-
-    lax.fori_loop(0, a_own.shape[1] // LANE_TILE, one_tile, 0)
-    for to, row, n, source in runs:
-        if direct or to > 0:
-            outs[to][pl.ds(row, n), pl.ds(a_own.shape[1], LANES)] = heads[source, :].astype(jnp.int16)
-
-
-def products(direct, sizes, table, operands, a_own, a_other):
-    rows, total = a_own.shape[1], sum(sizes)
-    if direct:
-        out_shape = [jax.ShapeDtypeStruct((16 * total, rows + LANES), jnp.int16)]
-    else:
-        out_shape = [jax.ShapeDtypeStruct((4 * total, rows), jnp.float32)] + [
-            jax.ShapeDtypeStruct((4 * total, rows + LANES), jnp.int16)
-        ] * 3
+        for to, into, source in runs:
+            ready[to][into, lanes] = acc[source, :] if to == kept else steps[source, :]
+        for to in range(n_outs):
+            leave(to, tile).start()
+    for to, into, source in runs:
+        if to != kept:
+            ready[to][into, pl.ds(columns, LANES)] = heads[source, :].astype(jnp.int16)
+    for to in range(n_outs):
+        if to != kept:
+            leave(to, tiles).start()
+    for to in range(n_outs):
+        for tile in range(tiles if to == kept else tiles + 1):
+            leave(to, tile).wait()
+
+
+def products(mode, sizes, table, operands, a_own, a_other):
+    (rows, depth), total = a_own.shape, sum(sizes)
+    tiles = rows // LANE_TILE
     arrays = []
     for array, _ in operands:
         if not any(array is known for known in arrays):
             arrays.append(array)
     where = [(next(i for i, known in enumerate(arrays) if known is array), row) for array, row in operands]
-    vmem = pl.BlockSpec(memory_space=pltpu.VMEM)
-    return pl.pallas_call(
-        functools.partial(product_kernel, direct, sizes, list(zip(where[::2], where[1::2])), len(arrays)),
-        out_shape=out_shape,
-        in_specs=[pl.BlockSpec(memory_space=pltpu.SMEM)] + [vmem] * (len(arrays) + 2),
-        out_specs=[vmem] * len(out_shape),
-        scratch_shapes=[
+    if mode == "direct":
+        shapes = [((16 * total, rows + LANES), jnp.int16)]
+    else:
+        shapes = [((4 * total, rows), jnp.float32)] + [((4 * total, rows + LANES), jnp.int16)] * 3
+    vmem, hbm = (pl.BlockSpec(memory_space=space) for space in (pltpu.VMEM, pltpu.HBM))
+    return pl.pallas_call(
+        functools.partial(product_kernel, mode, sizes, list(zip(where[::2], where[1::2])), len(arrays)),
+        out_shape=[pltpu.HBM(*shape) for shape in shapes],
+        in_specs=[pl.BlockSpec(memory_space=pltpu.SMEM)] + [vmem] * len(arrays) + [hbm] * 2,
+        out_specs=[hbm] * len(shapes),
+        scratch_shapes=[pltpu.VMEM(*shape) for shape in shapes]
+        + [
             pltpu.VMEM((16 * total, LANE_TILE), jnp.float32),
             pltpu.VMEM((16 * total, LANE_TILE), jnp.int16),
             pltpu.VMEM((16 * total, LANES), jnp.int32),
+            pltpu.VMEM((tiles, 2, LANE_TILE, depth), jnp.bfloat16),
+            pltpu.VMEM((2, 16 * total, depth), jnp.bfloat16),
+            pltpu.SemaphoreType.DMA((tiles, 2)),
+            pltpu.SemaphoreType.DMA((len(shapes), tiles + 1)),
         ],
         compiler_params=params(),
-        cost_estimate=cost(1.5 + total / 5),
-    )(table, *arrays, a_own, a_other)
+        cost_estimate=cost(1 + total / 6),
+    )(table, *arrays, *(pltpu.with_memory_space_constraint(half, pltpu.HBM) for half in (a_own, a_other)))
 
 
 def join_kernel(sizes, table, kept, one, two, three, *outs_and_scratch):
@@ -270,10 +304,10 @@
 PLANE_GROUPS = [[index_in_plane(y, z, core) for y in range(4) for z in range(4)] for core in range(2)]
 CHUNKS = (32, 16, 16)
 GROUPS = (
-    (True, (("near", 0),)),
-    (False, (("near", 1), ("far", 0))),
-    (False, (("near", 2), ("far", 1))),
-    (True, (("far", 2),)),
+    ("direct", (("near", 0),)),
+    ("steps", (("near", 1), ("far", 0))),
+    ("steps", (("near", 2), ("far", 1))),
+    ("direct", (("far", 2),)),
 )
 
 
@@ -290,11 +324,12 @@
     own = [[(cut(mine, j), 0), (cut(swapped, j), 0)] for j in range(len(CHUNKS))]
     join_all = lax.optimization_barrier
 
-    def send(forward, j):
+    def send(j):
+        held = lambda spot: lax.slice_in_dim(spot[0], spot[1], spot[1] + 8 * CHUNKS[j - 1])
         following = [own[j][0][0], own[j][1][0]] if j < len(CHUNKS) else []
         return (
-            shift(jnp.concatenate(forward[0] + following), dx=1),
-            shift(jnp.concatenate(forward[1] + following), dx=-1),
+            shift(jnp.concatenate([held(left[j - 1][0])] + following), dx=1),
+            shift(jnp.concatenate([held(right[j - 1][1])] + following), dx=-1),
         )
 
     left, right, far = [], [], []
@@ -307,27 +342,25 @@
             for side, array in zip((left, right), arrived):
                 side.append([(array, skip), (array, skip + 8 * CHUNKS[j])])
 
-    def forward(j):
-        held = lambda spot: lax.slice_in_dim(spot[0], spot[1], spot[1] + 8 * CHUNKS[j])
-        return [held(left[j][0])], [held(right[j][1])]
-
-    first = send(([], []), 0)
-    a_own = turned_amps(amps, after(amp_live, mine))
-    a_other = shift(a_own, dcore=1)
-    *first, a_own, a_other = join_all((*first, a_own, a_other))
+    own[0] = [(after(own[0][0][0], own[0][1][0]), 0), own[0][1]]
+    start = jnp.concatenate([own[0][0][0], own[0][1][0]])
+    first = shift(start, dx=1), shift(start, dx=-1)
+    live_other, amps_other = shift(amp_live, dcore=1), shift(amps, dcore=1)
+    a_both = masked_amps(after(amp_live, start), live_other, amps, amps_other)
+    *first, a_both = join_all((*first, a_both))
     receive(first, 0)
 
     def y_run(first_block, places):
         pair = jnp.where(places // 2 == (first_block % 4) // 2, 0, 1)
         return pair * 2 + places % 2
 
-    def spread(direct, parts, previous):
+    def spread(mode, parts, previous):
         sizes = tuple(CHUNKS[j] for _, j in parts)
         operands, tables, later = [], [], []
         for kind, j in parts:
             first = x - 1 if kind == "near" else x
             operands += left[j] + right[j] if kind == "near" else own[j] + far[j]
-            if direct:
+            if mode == "direct":
                 tables.append((y_run(first, around)[:, None] * 4 + around[None, :]).reshape(16))
             else:
                 z_to, y_to = (z + around) % 4, y_run(first, (y + around) % 4)
@@ -336,21 +369,21 @@
                 tables.append(jnp.where(core == 0, z_first, y_first).reshape(16))
                 later.append(jnp.where(core == 0, y_to, z_to))
         table = after(jnp.concatenate(tables).astype(jnp.int32), *previous)
-        if direct:
-            (sent,) = products(True, sizes, table, operands, a_own, a_other)
+        if mode == "direct":
+            (sent,) = products(mode, sizes, table, operands, *a_both)
             got = lax.all_to_all(sent, ("oj", "vert"), 0, 0, axis_index_groups=PLANE_GROUPS, tiled=True)
             return sum_of(got), [sent]
-        kept, *sent = products(False, sizes, table, operands, a_own, a_other)
+        kept, *sent = products(mode, sizes, table, operands, *a_both)
         at_once = sent
         arrived = [shift(s, dplane=((0, d + 1), (d + 1, 0))) for d, s in enumerate(sent)]
         kept, *sent = join(sizes, jnp.concatenate(later).astype(jnp.int32), kept, arrived)
         return last(kept, [shift(s, dplane=((d + 1, 0), (0, d + 1))) for d, s in enumerate(sent)]), at_once
 
     found, previous = {}, []
-    for j, (direct, parts) in enumerate(GROUPS):
+    for j, (mode, parts) in enumerate(GROUPS):
         if j < len(CHUNKS):
-            coming = send(forward(j), j + 1)
-        result, previous = spread(direct, parts, previous)
+            coming = send(j + 1)
+        result, previous = spread(mode, parts, previous)
         if j < len(CHUNKS):
             *coming, previous = join_all((*coming, previous))
             receive(coming, j + 1)

time: 168 us -> 160 us (0.952); the launches traced: 167 us -> 157 us
  waiting for transfers between devices: 45.1 us -> 32.3 us
  Pallas kernels: 55.4 us -> 57.4 us
  local copies, waits for them, and re-layouts: 20.3 us -> 18.6 us
    ppermute x23 -> x24, waiting for transfers between devices: 45.1 us -> 32.2 us  [shift(): return lax.ppermute(value, AXES, pairs)]
    unnamed x40 -> x31, local copies, waits for them, and re-layouts: 11.4 us -> 7.75 us
    ppermute x23 -> x24, starting transfers between devices: 25.9 us -> 28.8 us  [shift(): return lax.ppermute(value, AXES, pairs)]
    slice x6, local copies, waits for them, and re-layouts: 3.09 us -> 5.04 us  [send(): lax.slice_in_dim(spot[0], spot[1], spot[1] + 8 * CHUNKS[j - 1])]
    all_to_all x2, starting transfers between devices: 15.4 us -> 13.5 us  [spread(): lax.all_to_all(sent, ('oj', 'vert'), 0, 0, axis_index_groups=PLANE_GROUPS...]
    pallas_call x5, Pallas kernels: 45.5 us -> 47.2 us  [the longest x4 40.2 us: products(): pl.pallas_call(functools.partial(product_kernel, mode, sizes, list(zip(wh...]
  transfers between devices with their start and end apart: 25 -> 26, of which waited for: 9 -> 8; matrix products, arithmetic and copies ran while one was open for 5% -> 8% of each run, Pallas kernels for 29% -> 36%
where the time goes in v3:
time: 160 us; the launch traced here: 157 us
  Pallas kernels  57.4 us (36%)
  starting transfers between devices  42.4 us (26%)
  waiting for transfers between devices  32.3 us (20%)
  local copies, waits for them, and re-layouts  18.6 us (12%)
  other arithmetic  5.79 us (4%)
    pallas_call x4, Pallas kernels, products(): pl.pallas_call(functools.partial(product_kernel, mode, sizes, list(zip(wh...  40.2 us
    ppermute x24, waiting for transfers between devices, shift(): return lax.ppermute(value, AXES, pairs)  32.2 us
    ppermute x24, starting transfers between devices, shift(): return lax.ppermute(value, AXES, pairs)  28.8 us
    all_to_all x2, starting transfers between devices, spread(): lax.all_to_all(sent, ('oj', 'vert'), 0, 0, axis_index_groups=PLANE_GROUPS...  13.5 us
    unnamed x31, local copies, waits for them, and re-layouts  7.75 us
    pallas_call x1, Pallas kernels, masked_amps(): pl.pallas_call(masked_kernel, grid=(rows // LANE_TILE,), out_shape=[pltpu...  7.03 us
    pallas_call x2, Pallas kernels, join(): pl.pallas_call(functools.partial(join_kernel, sizes), out_shape=out_shape...  5.72 us
    slice x6, local copies, waits for them, and re-layouts, send(): lax.slice_in_dim(spot[0], spot[1], spot[1] + 8 * CHUNKS[j - 1])  5.04 us
  transfers between devices with their start and end apart: 26, of which 8 were waited for; matrix products, arithmetic and copies ran while one was open for 8% of the time, Pallas kernels for 36%

profile of v3, /device:TPU:1, one launch (start us, length us, event | category | flops | bytes accessed | tf_op | source)
XLA Modules:
  0.0 156.8 jit_solution(15270424796385753223)
XLA Ops:
  3.7 2.4 %shard_map.64 = (bf16[8,64,1024]{2,1,0:T(8,128)(2,1)S(1)}, bf16[8,64,1024]{2,1,0:T(8,128)(2,1)S(1)}) custom-call(s32[1]{0:T(128)} %bitcast.core, s32[8,8]{1,0:T(8,128)S(1)} %copy-done.9, bf16[1024,1024]{1,0:T(8,128)(2,1)S(1)} %copy-done.8), custom_call_target="tpu_custom_call" | custom-call | flops 2875000064 | bytes 1000 | tf_op jit(solution)/shard_map/pallas_call | solution.py:88
  7.7 2.1 %collective-permute-done = bf16[8,64,1024]{2,1,0:T(8,128)(2,1)} collective-permute-done((bf16[8,64,1024]{2,1,0:T(8,128)(2,1)S(1)}, bf16[8,64,1024]{2,1,0:T(8,128)(2,1)}, u32[]{:S(2)}, u32[]{:S(2)}) %collective-permute-start) | collective-permute-done | bytes 1048608 | tf_op jit(solution)/shard_map/ppermute | solution.py:37
  12.0 2.6 %collective-permute-start.2 = (bf16[512,1024]{1,0:T(8,128)(2,1)}, bf16[512,1024]{1,0:T(8,128)(2,1)S(1)}, u32[]{:S(2)}, u32[]{:S(2)}) collective-permute-start(bf16[512,1024]{1,0:T(8,128)(2,1)} %pad_maximum_fusion.4), channel_id=1, source_target_pairs={{0,96},{1,97},{2,98},{3,99},{4,100},{5,101},{6,102},{7,103},{8,104... | collective-permute-start | bytes 3145736 | tf_op jit(solution)/shard_map/ppermute | solution.py:37
  16.5 2.2 %copy-done.7 = bf16[2048,1024]{1,0:T(8,128)(2,1)S(1)} copy-done((bf16[2048,1024]{1,0:T(8,128)(2,1)S(1)}, bf16[2048,1024]{1,0:T(8,128)(2,1)}, u32[]{:S(2)}) %copy-start.7) | copy-done | bytes 4194328
  18.7 7.0 %shard_map.65 = (bf16[2048,1024]{1,0:T(8,128)(2,1)}, bf16[2048,1024]{1,0:T(8,128)(2,1)}) custom-call(s32[16,8]{1,0:T(8,128)S(1)} %copy.8.live_own, s32[16,8]{1,0:T(8,128)S(1)} %collective-permute-done.3.live_other, bf16[2048,1024]{1,0:T(8,128)(2,1)S(1)} %copy-done.7, bf16[2048,1024]{1,0:T(8,128)(2,1)} %collective-permute-done.4.other), custom_call_target="tpu_custom_call" | custom-call | flops 6899999744 | bytes 1000 | tf_op jit(solution)/shard_map/pallas_call | solution.py:114
  25.7 11.3 %collective-permute-done.2.refs_1_ = bf16[512,1024]{1,0:T(8,128)(2,1)S(1)} collective-permute-done((bf16[512,1024]{1,0:T(8,128)(2,1)}, bf16[512,1024]{1,0:T(8,128)(2,1)S(1)}, u32[]{:S(2)}, u32[]{:S(2)}) %collective-permute-start.2) | collective-permute-done | bytes 1048608 | tf_op jit(solution)/shard_map/ppermute | solution.py:37
  37.0 3.1 %collective-permute-done.1.refs_0_ = bf16[512,1024]{1,0:T(8,128)(2,1)} collective-permute-done((bf16[512,1024]{1,0:T(8,128)(2,1)}, bf16[512,1024]{1,0:T(8,128)(2,1)}, u32[]{:S(2)}, u32[]{:S(2)}) %collective-permute-start.1) | collective-permute-done | bytes 1048608 | tf_op jit(solution)/shard_map/ppermute | solution.py:37
  44.8 9.9 %shard_map.66 = s16[512,2176]{1,0:T(8,128)(2,1)} custom-call(s32[16]{0:T(128)S(1)} %add.331.table, bf16[512,1024]{1,0:T(8,128)(2,1)} %collective-permute-done.1.refs_0_, bf16[512,1024]{1,0:T(8,128)(2,1)S(1)} %collective-permute-done.2.refs_1_, bf16[2048,1024]{1,0:T(8,128)(2,1)} %get-tuple-element.45.refs_2_.refs_4_, ...), custom_call_target="tpu_custom_call" | custom-call | flops 7283333120 | bytes 1000 | tf_op jit(solution)/shard_map/pallas_call | solution.py:202
  54.7 7.8 %all-to-all-start.1 = ((s16[16,32,2176]{2,1,0:T(8,128)(2,1)}), s16[16,32,2176]{2,1,0:T(8,128)(2,1)S(1)}, u32[]{:S(2)}, u32[]{:S(2)}) async-start(s16[16,32,2176]{2,1,0:T(8,128)(2,1)} %bitcast.29), calls=%async_computation.1 | async-start | bytes 4456448 | tf_op jit(solution)/shard_map/all_to_all | solution.py:374
  62.5 3.8 %collective-permute-done.6.refs_1_ = bf16[512,1024]{1,0:T(8,128)(2,1)} collective-permute-done((bf16[512,1024]{1,0:T(8,128)(2,1)}, bf16[512,1024]{1,0:T(8,128)(2,1)}, u32[]{:S(2)}, u32[]{:S(2)}) %collective-permute-start.6) | collective-permute-done | bytes 1048608 | tf_op jit(solution)/shard_map/ppermute | solution.py:37
  69.7 2.4 %pad_maximum_fusion.5 = (bf16[384,1024]{1,0:T(8,128)(2,1)}, bf16[384,1024]{1,0:T(8,128)(2,1)}) fusion(bf16[128,1024]{1,0:T(8,128)(2,1)} %bitcast.27, bf16[128,1024]{1,0:T(8,128)(2,1)} %bitcast.25, bf16[128,1024]{1,0:T(8,128)(2,1)S(1)} %slice.58, bf16[128,1024]{1,0:T(8,128)(2,1)S(1)} %slice.55), kind=kLoop, calls=%fused_computation.8 | loop fusion | flops 3932160 | bytes 2621440 | tf_op jit(solution)/shard_map/concatenate | solution.py:332
  73.6 12.5 %shard_map.67 = (f32[192,2048]{1,0:T(8,128)}, s16[192,2176]{1,0:T(8,128)(2,1)}, s16[192,2176]{1,0:T(8,128)(2,1)}, s16[192,2176]{1,0:T(8,128)(2,1)}) custom-call(s32[32]{0:T(128)S(1)} %pad_add_fusion.1.table, bf16[512,1024]{1,0:T(8,128)(2,1)} %collective-permute-done.5.refs_0_, bf16[512,1024]{1,0:T(8,128)(2,1)} %collective-permute-done.6.refs_1_, ...), custom_call_target="tpu_custom_call" | custom-call | flops 10350000128 | bytes 1000 | tf_op jit(solution)/shard_map/pallas_call | solution.py:202
  87.6 2.6 %collective-permute-start.8 = (s16[192,2176]{1,0:T(8,128)(2,1)}, s16[192,2176]{1,0:T(8,128)(2,1)}, u32[]{:S(2)}, u32[]{:S(2)}) collective-permute-start(s16[192,2176]{1,0:T(8,128)(2,1)} %get-tuple-element.51), channel_id=1, source_target_pairs={{0,2},{1,3},{2,0},{3,1},{4,6},{5,7},{6,4},{7,5},{8,24},{9,25},{10,... | collective-permute-start | bytes 2506760 | tf_op jit(solution)/shard_map/ppermute | solution.py:37
  95.8 10.0 %shard_map.70 = (f32[128,2048]{1,0:T(8,128)}, s16[128,2176]{1,0:T(8,128)(2,1)}, s16[128,2176]{1,0:T(8,128)(2,1)}, s16[128,2176]{1,0:T(8,128)(2,1)}) custom-call(s32[32]{0:T(128)S(1)} %pad_add_fusion.1.table, bf16[384,1024]{1,0:T(8,128)(2,1)} %collective-permute-done.13.refs_0_, bf16[384,1024]{1,0:T(8,128)(2,1)} %collective-permute-done.14.refs_1_, ...), custom_call_target="tpu_custom_call" | custom-call | flops 7283333120 | bytes 1000 | tf_op jit(solution)/shard_map/pallas_call | solution.py:202
  106.4 2.6 %collective-permute-start.16 = (s16[128,2176]{1,0:T(8,128)(2,1)}, s16[128,2176]{1,0:T(8,128)(2,1)}, u32[]{:S(2)}, u32[]{:S(2)}) collective-permute-start(s16[128,2176]{1,0:T(8,128)(2,1)} %get-tuple-element.61), channel_id=1, source_target_pairs={{0,2},{1,3},{2,0},{3,1},{4,6},{5,7},{6,4},{7,5},{8,24},{9,25},{10,... | collective-permute-start | bytes 1671176 | tf_op jit(solution)/shard_map/ppermute | solution.py:37
  110.1 7.7 %shard_map.73 = s16[256,2176]{1,0:T(8,128)(2,1)} custom-call(s32[16]{0:T(128)S(1)} %add.336.table, bf16[128,1024]{1,0:T(8,128)(2,1)S(1)} %bitcast.26, bf16[128,1024]{1,0:T(8,128)(2,1)S(1)} %bitcast.28, bf16[128,1024]{1,0:T(8,128)(2,1)S(1)} %collective-permute-done.21.refs_2_, bf16[128,1024]{1,0:T(8,128)(2,1)S(1)} %collective-permute-done.22.refs_3_, ...), custom_call_target="tpu_custom_call" | custom-call | flops 4216666624 | bytes 1000 | tf_op jit(solution)/shard_map/pallas_call | solution.py:202
  117.9 5.7 %all-to-all-start = ((s16[16,16,2176]{2,1,0:T(8,128)(2,1)}), s16[16,16,2176]{2,1,0:T(8,128)(2,1)S(1)}, u32[]{:S(2)}, u32[]{:S(2)}) async-start(s16[16,16,2176]{2,1,0:T(8,128)(2,1)} %bitcast.30), calls=%async_computation | async-start | bytes 2228224 | tf_op jit(solution)/shard_map/all_to_all | solution.py:374
  125.1 3.2 %shard_map.68 = (f32[48,2048]{1,0:T(8,128)S(1)}, s16[48,2176]{1,0:T(8,128)(2,1)S(1)}, s16[48,2176]{1,0:T(8,128)(2,1)S(1)}, s16[48,2176]{1,0:T(8,128)(2,1)S(1)}) custom-call(s32[8]{0:T(128)S(1)} %pad_add_fusion.table, f32[192,2048]{1,0:T(8,128)S(1)} %copy-done.10, s16[192,2176]{1,0:T(8,128)(2,1)} %collective-permute-done.7.one, ...), custom_call_target="tpu_custom_call" | custom-call | flops 2644999936 | bytes 1000 | tf_op jit(solution)/shard_map/pallas_call | solution.py:249
  129.7 2.4 %collective-permute-start.11 = (s16[48,2176]{1,0:T(8,128)(2,1)S(1)}, s16[48,2176]{1,0:T(8,128)(2,1)S(1)}, u32[]{:S(2)}, u32[]{:S(2)}) collective-permute-start(s16[48,2176]{1,0:T(8,128)(2,1)S(1)} %get-tuple-element.55), channel_id=1, source_target_pairs={{0,16},{1,17},{2,18},{3,19},{4,20},{5,21},{6,22},{7,23},{8,10},{9,... | collective-permute-start | bytes 626696 | tf_op jit(solution)/shard_map/ppermute | solution.py:37
  133.3 2.5 %shard_map.71 = (f32[32,2048]{1,0:T(8,128)S(1)}, s16[32,2176]{1,0:T(8,128)(2,1)S(1)}, s16[32,2176]{1,0:T(8,128)(2,1)S(1)}, s16[32,2176]{1,0:T(8,128)(2,1)S(1)}) custom-call(s32[8]{0:T(128)S(1)} %pad_add_fusion.table, f32[128,2048]{1,0:T(8,128)S(1)} %copy-done.11, s16[128,2176]{1,0:T(8,128)(2,1)} %collective-permute-done.15.one, ...), custom_call_target="tpu_custom_call" | custom-call | flops 2644999936 | bytes 1000 | tf_op jit(solution)/shard_map/pallas_call | solution.py:249
  137.1 6.0 %collective-permute-done.10.one = s16[48,2176]{1,0:T(8,128)(2,1)S(1)} collective-permute-done((s16[48,2176]{1,0:T(8,128)(2,1)S(1)}, s16[48,2176]{1,0:T(8,128)(2,1)S(1)}, u32[]{:S(2)}, u32[]{:S(2)}) %collective-permute-start.10) | collective-permute-done | bytes 208928 | tf_op jit(solution)/shard_map/ppermute | solution.py:37
  143.1 1.8 %collective-permute-start.20 = (s16[32,2176]{1,0:T(8,128)(2,1)S(1)}, s16[32,2176]{1,0:T(8,128)(2,1)S(1)}, u32[]{:S(2)}, u32[]{:S(2)}) collective-permute-start(s16[32,2176]{1,0:T(8,128)(2,1)S(1)} %get-tuple-element.66), channel_id=1, source_target_pairs={{0,20},{1,21},{2,22},{3,23},{4,0},{5,1},{6,2},{7,3},{8,11},{9,8},{... | collective-permute-start | bytes 417800 | tf_op jit(solution)/shard_map/ppermute | solution.py:37
  147.0 2.9 %collective-permute-done.19.two = s16[32,2176]{1,0:T(8,128)(2,1)S(1)} collective-permute-done((s16[32,2176]{1,0:T(8,128)(2,1)S(1)}, s16[32,2176]{1,0:T(8,128)(2,1)S(1)}, u32[]{:S(2)}, u32[]{:S(2)}) %collective-permute-start.19) | collective-permute-done | bytes 139296 | tf_op jit(solution)/shard_map/ppermute | solution.py:37
  151.3 2.4 %collective-permute-start.23 = (f32[64,2048]{1,0:T(8,128)S(1)}, f32[64,2048]{1,0:T(8,128)S(1)}, u32[]{:S(2)}, u32[]{:S(2)}) collective-permute-start(f32[64,2048]{1,0:T(8,128)S(1)} %get-tuple-element.70), channel_id=1, source_target_pairs={{0,8},{1,9},{2,10},{3,11},{4,12},{5,13},{6,14},{7,15},{8,0},{9,1},... | collective-permute-start | bytes 1572872 | tf_op jit(solution)/shard_map/ppermute | solution.py:37
  (106 shorter events, 39.4 us)
Async XLA Ops:
  0.0 16.5 %collective-permute-start.4 = (bf16[2048,1024]{1,0:T(8,128)(2,1)}, bf16[2048,1024]{1,0:T(8,128)(2,1)}, u32[]{:S(2)}, u32[]{:S(2)}) collective-permute-start(bf16[2048,1024]{1,0:T(8,128)(2,1)} %own.1), channel_id=1, source_target_pairs={{0,8},{1,9},{2,10},{3,11},{4,12},{5,13},{6,14},{7,15},{8,0},{9,1},... | collective-permute-start | bytes 12582920 | tf_op jit(solution)/shard_map/ppermute | solution.py:37
  6.3 10.1 %collective-permute-start.3 = (s32[16,8]{1,0:T(8,128)S(1)}, s32[16,8]{1,0:T(8,128)S(1)}, u32[]{:S(2)}, u32[]{:S(2)}) collective-permute-start(s32[16,8]{1,0:T(8,128)S(1)} %copy.7), channel_id=1, source_target_pairs={{0,8},{1,9},{2,10},{3,11},{4,12},{5,13},{6,14},{7,15},{8,0},{9,1},... | collective-permute-start | bytes 1544 | tf_op jit(solution)/shard_map/ppermute | solution.py:37
  12.0 25.1 %collective-permute-start.2 = (bf16[512,1024]{1,0:T(8,128)(2,1)}, bf16[512,1024]{1,0:T(8,128)(2,1)S(1)}, u32[]{:S(2)}, u32[]{:S(2)}) collective-permute-start(bf16[512,1024]{1,0:T(8,128)(2,1)} %pad_maximum_fusion.4), channel_id=1, source_target_pairs={{0,96},{1,97},{2,98},{3,99},{4,100},{5,101},{6,102},{7,103},{8,104... | collective-permute-start | bytes 3145736 | tf_op jit(solution)/shard_map/ppermute | solution.py:37
  14.5 25.6 %collective-permute-start.1 = (bf16[512,1024]{1,0:T(8,128)(2,1)}, bf16[512,1024]{1,0:T(8,128)(2,1)}, u32[]{:S(2)}, u32[]{:S(2)}) collective-permute-start(bf16[512,1024]{1,0:T(8,128)(2,1)} %pad_maximum_fusion.4), channel_id=1, source_target_pairs={{0,32},{1,33},{2,34},{3,35},{4,36},{5,37},{6,38},{7,39},{8,40},{9,... | collective-permute-start | bytes 3145736 | tf_op jit(solution)/shard_map/ppermute | solution.py:37
  42.9 23.4 %collective-permute-start.6 = (bf16[512,1024]{1,0:T(8,128)(2,1)}, bf16[512,1024]{1,0:T(8,128)(2,1)}, u32[]{:S(2)}, u32[]{:S(2)}) collective-permute-start(bf16[512,1024]{1,0:T(8,128)(2,1)} %get-tuple-element.77), channel_id=1, source_target_pairs={{0,96},{1,97},{2,98},{3,99},{4,100},{5,101},{6,102},{7,103},{8,104... | collective-permute-start | bytes 3145736 | tf_op jit(solution)/shard_map/ppermute | solution.py:37
  43.1 24.7 %collective-permute-start.5 = (bf16[512,1024]{1,0:T(8,128)(2,1)}, bf16[512,1024]{1,0:T(8,128)(2,1)}, u32[]{:S(2)}, u32[]{:S(2)}) collective-permute-start(bf16[512,1024]{1,0:T(8,128)(2,1)} %get-tuple-element.78), channel_id=1, source_target_pairs={{0,32},{1,33},{2,34},{3,35},{4,36},{5,37},{6,38},{7,39},{8,40},{9,... | collective-permute-start | bytes 3145736 | tf_op jit(solution)/shard_map/ppermute | solution.py:37
  54.7 63.1 %all-to-all-start.1 = ((s16[16,32,2176]{2,1,0:T(8,128)(2,1)}), s16[16,32,2176]{2,1,0:T(8,128)(2,1)S(1)}, u32[]{:S(2)}, u32[]{:S(2)}) async-start(s16[16,32,2176]{2,1,0:T(8,128)(2,1)} %bitcast.29), calls=%async_computation.1 | async-start | bytes 4456448 | tf_op jit(solution)/shard_map/all_to_all | solution.py:374
  72.1 19.2 %collective-permute-start.14 = (bf16[384,1024]{1,0:T(8,128)(2,1)}, bf16[384,1024]{1,0:T(8,128)(2,1)}, u32[]{:S(2)}, u32[]{:S(2)}) collective-permute-start(bf16[384,1024]{1,0:T(8,128)(2,1)} %get-tuple-element.75), channel_id=1, source_target_pairs={{0,96},{1,97},{2,98},{3,99},{4,100},{5,101},{6,102},{7,103},{8,104... | collective-permute-start | bytes 2359304 | tf_op jit(solution)/shard_map/ppermute | solution.py:37
  72.4 18.9 %collective-permute-start.13 = (bf16[384,1024]{1,0:T(8,128)(2,1)}, bf16[384,1024]{1,0:T(8,128)(2,1)}, u32[]{:S(2)}, u32[]{:S(2)}) collective-permute-start(bf16[384,1024]{1,0:T(8,128)(2,1)} %get-tuple-element.76), channel_id=1, source_target_pairs={{0,32},{1,33},{2,34},{3,35},{4,36},{5,37},{6,38},{7,39},{8,40},{9,... | collective-permute-start | bytes 2359304 | tf_op jit(solution)/shard_map/ppermute | solution.py:37
  86.0 23.0 %collective-permute-start.7 = (s16[192,2176]{1,0:T(8,128)(2,1)}, s16[192,2176]{1,0:T(8,128)(2,1)}, u32[]{:S(2)}, u32[]{:S(2)}) collective-permute-start(s16[192,2176]{1,0:T(8,128)(2,1)} %get-tuple-element.50), channel_id=1, source_target_pairs={{0,1},{1,2},{2,3},{3,0},{4,5},{5,6},{6,7},{7,4},{8,12},{9,13},{10,... | collective-permute-start | bytes 2506760 | tf_op jit(solution)/shard_map/ppermute | solution.py:37
  87.6 36.0 %collective-permute-start.8 = (s16[192,2176]{1,0:T(8,128)(2,1)}, s16[192,2176]{1,0:T(8,128)(2,1)}, u32[]{:S(2)}, u32[]{:S(2)}) collective-permute-start(s16[192,2176]{1,0:T(8,128)(2,1)} %get-tuple-element.51), channel_id=1, source_target_pairs={{0,2},{1,3},{2,0},{3,1},{4,6},{5,7},{6,4},{7,5},{8,24},{9,25},{10,... | collective-permute-start | bytes 2506760 | tf_op jit(solution)/shard_map/ppermute | solution.py:37
  90.2 33.4 %collective-permute-start.9 = (s16[192,2176]{1,0:T(8,128)(2,1)}, s16[192,2176]{1,0:T(8,128)(2,1)}, u32[]{:S(2)}, u32[]{:S(2)}) collective-permute-start(s16[192,2176]{1,0:T(8,128)(2,1)} %get-tuple-element.52), channel_id=1, source_target_pairs={{0,3},{1,0},{2,1},{3,2},{4,7},{5,4},{6,5},{7,6},{8,28},{9,29},{10,... | collective-permute-start | bytes 2506760 | tf_op jit(solution)/shard_map/ppermute | solution.py:37
  93.3 12.5 %collective-permute-start.22 = (bf16[128,1024]{1,0:T(8,128)(2,1)S(1)}, bf16[128,1024]{1,0:T(8,128)(2,1)S(1)}, u32[]{:S(2)}, u32[]{:S(2)}) collective-permute-start(bf16[128,1024]{1,0:T(8,128)(2,1)S(1)} %slice.61), channel_id=1, source_target_pairs={{0,96},{1,97},{2,98},{3,99},{4,100},{5,101},{6,102},{7,103},{8,104... | collective-permute-start | bytes 786440 | tf_op jit(solution)/shard_map/ppermute | solution.py:37
  94.9 11.5 %collective-permute-start.21 = (bf16[128,1024]{1,0:T(8,128)(2,1)S(1)}, bf16[128,1024]{1,0:T(8,128)(2,1)S(1)}, u32[]{:S(2)}, u32[]{:S(2)}) collective-permute-start(bf16[128,1024]{1,0:T(8,128)(2,1)S(1)} %slice.60), channel_id=1, source_target_pairs={{0,32},{1,33},{2,34},{3,35},{4,36},{5,37},{6,38},{7,39},{8,40},{9,... | collective-permute-start | bytes 786440 | tf_op jit(solution)/shard_map/ppermute | solution.py:37
  105.9 26.3 %collective-permute-start.15 = (s16[128,2176]{1,0:T(8,128)(2,1)}, s16[128,2176]{1,0:T(8,128)(2,1)}, u32[]{:S(2)}, u32[]{:S(2)}) collective-permute-start(s16[128,2176]{1,0:T(8,128)(2,1)} %get-tuple-element.60), channel_id=1, source_target_pairs={{0,1},{1,2},{2,3},{3,0},{4,5},{5,6},{6,7},{7,4},{8,12},{9,13},{10,... | collective-permute-start | bytes 1671176 | tf_op jit(solution)/shard_map/ppermute | solution.py:37
  106.4 26.9 %collective-permute-start.16 = (s16[128,2176]{1,0:T(8,128)(2,1)}, s16[128,2176]{1,0:T(8,128)(2,1)}, u32[]{:S(2)}, u32[]{:S(2)}) collective-permute-start(s16[128,2176]{1,0:T(8,128)(2,1)} %get-tuple-element.61), channel_id=1, source_target_pairs={{0,2},{1,3},{2,0},{3,1},{4,6},{5,7},{6,4},{7,5},{8,24},{9,25},{10,... | collective-permute-start | bytes 1671176 | tf_op jit(solution)/shard_map/ppermute | solution.py:37
  109.0 24.3 %collective-permute-start.17 = (s16[128,2176]{1,0:T(8,128)(2,1)}, s16[128,2176]{1,0:T(8,128)(2,1)}, u32[]{:S(2)}, u32[]{:S(2)}) collective-permute-start(s16[128,2176]{1,0:T(8,128)(2,1)} %get-tuple-element.62), channel_id=1, source_target_pairs={{0,3},{1,0},{2,1},{3,2},{4,7},{5,4},{6,5},{7,6},{8,28},{9,29},{10,... | collective-permute-start | bytes 1671176 | tf_op jit(solution)/shard_map/ppermute | solution.py:37
  117.9 32.2 %all-to-all-start = ((s16[16,16,2176]{2,1,0:T(8,128)(2,1)}), s16[16,16,2176]{2,1,0:T(8,128)(2,1)S(1)}, u32[]{:S(2)}, u32[]{:S(2)}) async-start(s16[16,16,2176]{2,1,0:T(8,128)(2,1)} %bitcast.30), calls=%async_computation | async-start | bytes 2228224 | tf_op jit(solution)/shard_map/all_to_all | solution.py:374
  128.3 14.8 %collective-permute-start.10 = (s16[48,2176]{1,0:T(8,128)(2,1)S(1)}, s16[48,2176]{1,0:T(8,128)(2,1)S(1)}, u32[]{:S(2)}, u32[]{:S(2)}) collective-permute-start(s16[48,2176]{1,0:T(8,128)(2,1)S(1)} %get-tuple-element.54), channel_id=1, source_target_pairs={{0,4},{1,5},{2,6},{3,7},{4,16},{5,17},{6,18},{7,19},{8,9},{9,10},{... | collective-permute-start | bytes 626696 | tf_op jit(solution)/shard_map/ppermute | solution.py:37
  129.7 16.9 %collective-permute-start.11 = (s16[48,2176]{1,0:T(8,128)(2,1)S(1)}, s16[48,2176]{1,0:T(8,128)(2,1)S(1)}, u32[]{:S(2)}, u32[]{:S(2)}) collective-permute-start(s16[48,2176]{1,0:T(8,128)(2,1)S(1)} %get-tuple-element.55), channel_id=1, source_target_pairs={{0,16},{1,17},{2,18},{3,19},{4,20},{5,21},{6,22},{7,23},{8,10},{9,... | collective-permute-start | bytes 626696 | tf_op jit(solution)/shard_map/ppermute | solution.py:37
  132.1 14.5 %collective-permute-start.12 = (s16[48,2176]{1,0:T(8,128)(2,1)S(1)}, s16[48,2176]{1,0:T(8,128)(2,1)S(1)}, u32[]{:S(2)}, u32[]{:S(2)}) collective-permute-start(s16[48,2176]{1,0:T(8,128)(2,1)S(1)} %get-tuple-element.56), channel_id=1, source_target_pairs={{0,20},{1,21},{2,22},{3,23},{4,0},{5,1},{6,2},{7,3},{8,11},{9,8},{... | collective-permute-start | bytes 626696 | tf_op jit(solution)/shard_map/ppermute | solution.py:37
  135.8 11.2 %collective-permute-start.18 = (s16[32,2176]{1,0:T(8,128)(2,1)S(1)}, s16[32,2176]{1,0:T(8,128)(2,1)S(1)}, u32[]{:S(2)}, u32[]{:S(2)}) collective-permute-start(s16[32,2176]{1,0:T(8,128)(2,1)S(1)} %get-tuple-element.64), channel_id=1, source_target_pairs={{0,4},{1,5},{2,6},{3,7},{4,16},{5,17},{6,18},{7,19},{8,9},{9,10},{... | collective-permute-start | bytes 417800 | tf_op jit(solution)/shard_map/ppermute | solution.py:37
  136.2 13.7 %collective-permute-start.19 = (s16[32,2176]{1,0:T(8,128)(2,1)S(1)}, s16[32,2176]{1,0:T(8,128)(2,1)S(1)}, u32[]{:S(2)}, u32[]{:S(2)}) collective-permute-start(s16[32,2176]{1,0:T(8,128)(2,1)S(1)} %get-tuple-element.65), channel_id=1, source_target_pairs={{0,16},{1,17},{2,18},{3,19},{4,20},{5,21},{6,22},{7,23},{8,10},{9,... | collective-permute-start | bytes 417800 | tf_op jit(solution)/shard_map/ppermute | solution.py:37
  143.1 6.8 %collective-permute-start.20 = (s16[32,2176]{1,0:T(8,128)(2,1)S(1)}, s16[32,2176]{1,0:T(8,128)(2,1)S(1)}, u32[]{:S(2)}, u32[]{:S(2)}) collective-permute-start(s16[32,2176]{1,0:T(8,128)(2,1)S(1)} %get-tuple-element.66), channel_id=1, source_target_pairs={{0,20},{1,21},{2,22},{3,23},{4,0},{5,1},{6,2},{7,3},{8,11},{9,8},{... | collective-permute-start | bytes 417800 | tf_op jit(solution)/shard_map/ppermute | solution.py:37
  (19 other events, 101.8 us)

commit v4 on v3

--- a/solution.py
+++ b/solution.py
@@ -141,7 +141,8 @@
         )
 
     def leave(out, tile):
-        lanes = pl.ds(tile * LANE_TILE, LANE_TILE if tile < tiles else LANES)
+        last = tile == tiles - 1 and out != kept
+        lanes = pl.ds(tile * LANE_TILE, LANE_TILE + LANES if last else LANE_TILE)
         return pltpu.make_async_copy(ready[out].at[:, lanes], outs[out].at[:, lanes], out_sems.at[out, tile])
 
     for half in range(2):
@@ -169,20 +170,21 @@
             fetch(tile, half).wait()
             if tile + 1 < tiles:
                 fetch(tile + 1, half).start()
-        acc[...] = dot_rows(blocks[0], amps[tile, 0]) + dot_rows(blocks[1], amps[tile, 1])
+            if tile == 0 and half == 0:
+                acc[...] = dot_rows(blocks[0], amps[0, 0])
+        if tile == 0:
+            acc[...] += dot_rows(blocks[1], amps[0, 1])
+        else:
+            acc[...] = dot_rows(blocks[0], amps[tile, 0]) + dot_rows(blocks[1], amps[tile, 1])
         encode(acc, steps, heads, tile)
         for to, into, source in runs:
             ready[to][into, lanes] = acc[source, :] if to == kept else steps[source, :]
+            if tile == tiles - 1 and to != kept:
+                ready[to][into, pl.ds(columns, LANES)] = heads[source, :].astype(jnp.int16)
         for to in range(n_outs):
             leave(to, tile).start()
-    for to, into, source in runs:
-        if to != kept:
-            ready[to][into, pl.ds(columns, LANES)] = heads[source, :].astype(jnp.int16)
     for to in range(n_outs):
-        if to != kept:
-            leave(to, tiles).start()
-    for to in range(n_outs):
-        for tile in range(tiles if to == kept else tiles + 1):
+        for tile in range(tiles):
             leave(to, tile).wait()
 
 
@@ -212,7 +214,7 @@
             pltpu.VMEM((tiles, 2, LANE_TILE, depth), jnp.bfloat16),
             pltpu.VMEM((2, 16 * total, depth), jnp.bfloat16),
             pltpu.SemaphoreType.DMA((tiles, 2)),
-            pltpu.SemaphoreType.DMA((len(shapes), tiles + 1)),
+            pltpu.SemaphoreType.DMA((len(shapes), tiles)),
         ],
         compiler_params=params(),
         cost_estimate=cost(1 + total / 6),
@@ -321,12 +323,13 @@
     starts = [sum(CHUNKS[:j]) for j in range(len(CHUNKS))]
     cut = lambda half, j: half[:, starts[j]:starts[j] + CHUNKS[j]].reshape(-1, depth)
     swapped = shift(theirs, dcore=1)
-    own = [[(cut(mine, j), 0), (cut(swapped, j), 0)] for j in range(len(CHUNKS))]
+    stacked = [jnp.concatenate([cut(mine, j), cut(swapped, j)]) for j in range(len(CHUNKS))]
+    own = [[(stacked[j], 0), (stacked[j], 8 * CHUNKS[j])] for j in range(len(CHUNKS))]
     join_all = lax.optimization_barrier
 
     def send(j):
         held = lambda spot: lax.slice_in_dim(spot[0], spot[1], spot[1] + 8 * CHUNKS[j - 1])
-        following = [own[j][0][0], own[j][1][0]] if j < len(CHUNKS) else []
+        following = [stacked[j]] if j < len(CHUNKS) else []
         return (
             shift(jnp.concatenate([held(left[j - 1][0])] + following), dx=1),
             shift(jnp.concatenate([held(right[j - 1][1])] + following), dx=-1),
@@ -342,11 +345,10 @@
             for side, array in zip((left, right), arrived):
                 side.append([(array, skip), (array, skip + 8 * CHUNKS[j])])
 
-    own[0] = [(after(own[0][0][0], own[0][1][0]), 0), own[0][1]]
-    start = jnp.concatenate([own[0][0][0], own[0][1][0]])
+    start = stacked[0]
     first = shift(start, dx=1), shift(start, dx=-1)
     live_other, amps_other = shift(amp_live, dcore=1), shift(amps, dcore=1)
-    a_both = masked_amps(after(amp_live, start), live_other, amps, amps_other)
+    a_both = masked_amps(after(amp_live, *stacked), live_other, amps, amps_other)
     *first, a_both = join_all((*first, a_both))
     receive(first, 0)
 

time: 160 us -> 156 us (0.975); the launches traced: 157 us -> 154 us
    slice x4, local copies, waits for them, and re-layouts: 3.64 us -> 1.01 us  [per_device(): half[:, starts[j]:starts[j] + CHUNKS[j]].reshape(-1, depth)]
    unnamed x31 -> x49, local copies, waits for them, and re-layouts: 7.75 us -> 9.91 us
  transfers between devices with their start and end apart: 26 -> 26, of which waited for: 8 -> 8; matrix products, arithmetic and copies ran while one was open for 8% -> 6% of each run, Pallas kernels for 36% -> 36%
where the time goes in v4:
time: 156 us; the launch traced here: 154 us
  Pallas kernels  56.6 us (36%)
  starting transfers between devices  42.1 us (27%)
  waiting for transfers between devices  31.9 us (20%)
  local copies, waits for them, and re-layouts  17.1 us (11%)
  other arithmetic  6.39 us (4%)
    pallas_call x4, Pallas kernels, products(): pl.pallas_call(functools.partial(product_kernel, mode, sizes, list(zip(wh...  39.6 us
    ppermute x24, waiting for transfers between devices, shift(): return lax.ppermute(value, AXES, pairs)  31.9 us
    ppermute x24, starting transfers between devices, shift(): return lax.ppermute(value, AXES, pairs)  28.6 us
    all_to_all x2, starting transfers between devices, spread(): lax.all_to_all(sent, ('oj', 'vert'), 0, 0, axis_index_groups=PLANE_GROUPS...  13.5 us
    unnamed x49, local copies, waits for them, and re-layouts  9.91 us
    pallas_call x1, Pallas kernels, masked_amps(): pl.pallas_call(masked_kernel, grid=(rows // LANE_TILE,), out_shape=[pltpu...  6.95 us
    pallas_call x2, Pallas kernels, join(): pl.pallas_call(functools.partial(join_kernel, sizes), out_shape=out_shape...  5.48 us
    slice x6, local copies, waits for them, and re-layouts, send(): lax.slice_in_dim(spot[0], spot[1], spot[1] + 8 * CHUNKS[j - 1])  3.94 us
  transfers between devices with their start and end apart: 26, of which 8 were waited for; matrix products, arithmetic and copies ran while one was open for 6% of the time, Pallas kernels for 36%

profile of v4, /device:TPU:1, one launch (start us, length us, event | category | flops | bytes accessed | tf_op | source)
XLA Modules:
  0.0 154.5 jit_solution(14181929040282374221)
XLA Ops:
  1.4 1.6 %copy-done.6 = bf16[1024,1024]{1,0:T(8,128)(2,1)S(1)} copy-done((bf16[1024,1024]{1,0:T(8,128)(2,1)S(1)}, bf16[1024,1024]{1,0:T(8,128)(2,1)}, u32[]{:S(2)}) %copy-start.6) | copy-done | bytes 2097176
  3.7 2.4 %shard_map.64 = (bf16[8,64,1024]{2,1,0:T(8,128)(2,1)S(1)}, bf16[8,64,1024]{2,1,0:T(8,128)(2,1)S(1)}) custom-call(s32[1]{0:T(128)} %bitcast.core, s32[8,8]{1,0:T(8,128)S(1)} %copy-done.9, bf16[1024,1024]{1,0:T(8,128)(2,1)S(1)} %copy-done.6), custom_call_target="tpu_custom_call" | custom-call | flops 2875000064 | bytes 1000 | tf_op jit(solution)/shard_map/pallas_call | solution.py:88
  10.8 2.6 %collective-permute-start.2 = (bf16[512,1024]{1,0:T(8,128)(2,1)S(1)}, bf16[512,1024]{1,0:T(8,128)(2,1)S(1)}, u32[]{:S(2)}, u32[]{:S(2)}) collective-permute-start(bf16[512,1024]{1,0:T(8,128)(2,1)S(1)} %pad_maximum_fusion.4.refs_2_), channel_id=1, source_target_pairs={{0,96},{1,97},{2,98},{3,99},{4,100},{5,101},{6,102},{7,103},{8,104... | collective-permute-start | bytes 3145736 | tf_op jit(solution)/shard_map/ppermute | solution.py:37
  14.7 2.2 %copy-done.5 = bf16[2048,1024]{1,0:T(8,128)(2,1)S(1)} copy-done((bf16[2048,1024]{1,0:T(8,128)(2,1)S(1)}, bf16[2048,1024]{1,0:T(8,128)(2,1)}, u32[]{:S(2)}) %copy-start.5) | copy-done | bytes 4194328
  16.9 7.0 %shard_map.65 = (bf16[2048,1024]{1,0:T(8,128)(2,1)}, bf16[2048,1024]{1,0:T(8,128)(2,1)}) custom-call(s32[16,8]{1,0:T(8,128)S(1)} %copy.8.live_own, s32[16,8]{1,0:T(8,128)S(1)} %collective-permute-done.3.live_other, bf16[2048,1024]{1,0:T(8,128)(2,1)S(1)} %copy-done.5, bf16[2048,1024]{1,0:T(8,128)(2,1)} %collective-permute-done.4.other), custom_call_target="tpu_custom_call" | custom-call | flops 6899999744 | bytes 1000 | tf_op jit(solution)/shard_map/pallas_call | solution.py:114
  23.9 11.7 %collective-permute-done.2.refs_1_ = bf16[512,1024]{1,0:T(8,128)(2,1)S(1)} collective-permute-done((bf16[512,1024]{1,0:T(8,128)(2,1)S(1)}, bf16[512,1024]{1,0:T(8,128)(2,1)S(1)}, u32[]{:S(2)}, u32[]{:S(2)}) %collective-permute-start.2) | collective-permute-done | bytes 1048608 | tf_op jit(solution)/shard_map/ppermute | solution.py:37
  35.6 3.1 %collective-permute-done.1.refs_0_ = bf16[512,1024]{1,0:T(8,128)(2,1)S(1)} collective-permute-done((bf16[512,1024]{1,0:T(8,128)(2,1)S(1)}, bf16[512,1024]{1,0:T(8,128)(2,1)S(1)}, u32[]{:S(2)}, u32[]{:S(2)}) %collective-permute-start.1) | collective-permute-done | bytes 1048608 | tf_op jit(solution)/shard_map/ppermute | solution.py:37
  42.3 9.4 %shard_map.66 = s16[512,2176]{1,0:T(8,128)(2,1)} custom-call(s32[16]{0:T(128)S(1)} %add.331.table, bf16[512,1024]{1,0:T(8,128)(2,1)S(1)} %collective-permute-done.1.refs_0_, bf16[512,1024]{1,0:T(8,128)(2,1)S(1)} %collective-permute-done.2.refs_1_, bf16[2048,1024]{1,0:T(8,128)(2,1)} %get-tuple-element.43.refs_2_.refs_3_, ...), custom_call_target="tpu_custom_call" | custom-call | flops 7283333120 | bytes 1000 | tf_op jit(solution)/shard_map/pallas_call | solution.py:204
  51.7 7.9 %all-to-all-start.1 = ((s16[16,32,2176]{2,1,0:T(8,128)(2,1)}), s16[16,32,2176]{2,1,0:T(8,128)(2,1)S(1)}, u32[]{:S(2)}, u32[]{:S(2)}) async-start(s16[16,32,2176]{2,1,0:T(8,128)(2,1)} %bitcast.25), calls=%async_computation.1 | async-start | bytes 4456448 | tf_op jit(solution)/shard_map/all_to_all | solution.py:376
  59.6 4.2 %collective-permute-done.6.refs_1_ = bf16[512,1024]{1,0:T(8,128)(2,1)} collective-permute-done((bf16[512,1024]{1,0:T(8,128)(2,1)}, bf16[512,1024]{1,0:T(8,128)(2,1)}, u32[]{:S(2)}, u32[]{:S(2)}) %collective-permute-start.6) | collective-permute-done | bytes 1048608 | tf_op jit(solution)/shard_map/ppermute | solution.py:37
  63.8 1.6 %collective-permute-done.5.refs_0_ = bf16[512,1024]{1,0:T(8,128)(2,1)} collective-permute-done((bf16[512,1024]{1,0:T(8,128)(2,1)}, bf16[512,1024]{1,0:T(8,128)(2,1)}, u32[]{:S(2)}, u32[]{:S(2)}) %collective-permute-start.5) | collective-permute-done | bytes 1048608 | tf_op jit(solution)/shard_map/ppermute | solution.py:37
  67.3 2.3 %pad_maximum_fusion.5 = (bf16[384,1024]{1,0:T(8,128)(2,1)}, bf16[384,1024]{1,0:T(8,128)(2,1)}) fusion(bf16[128,1024]{1,0:T(8,128)(2,1)} %bitcast.24, bf16[128,1024]{1,0:T(8,128)(2,1)S(1)} %bitcast.22, bf16[128,1024]{1,0:T(8,128)(2,1)S(1)} %slice.58, bf16[128,1024]{1,0:T(8,128)(2,1)S(1)} %slice.57), kind=kLoop, calls=%fused_computation.8 | loop fusion | flops 3932160 | bytes 2621440 | tf_op jit(solution)/shard_map/concatenate | solution.py:335
  71.1 12.4 %shard_map.67 = (f32[192,2048]{1,0:T(8,128)}, s16[192,2176]{1,0:T(8,128)(2,1)}, s16[192,2176]{1,0:T(8,128)(2,1)}, s16[192,2176]{1,0:T(8,128)(2,1)}) custom-call(s32[32]{0:T(128)S(1)} %pad_add_fusion.1.table, bf16[512,1024]{1,0:T(8,128)(2,1)} %collective-permute-done.5.refs_0_, bf16[512,1024]{1,0:T(8,128)(2,1)} %collective-permute-done.6.refs_1_, ...), custom_call_target="tpu_custom_call" | custom-call | flops 10350000128 | bytes 1000 | tf_op jit(solution)/shard_map/pallas_call | solution.py:204
  85.0 2.6 %collective-permute-start.8 = (s16[192,2176]{1,0:T(8,128)(2,1)}, s16[192,2176]{1,0:T(8,128)(2,1)}, u32[]{:S(2)}, u32[]{:S(2)}) collective-permute-start(s16[192,2176]{1,0:T(8,128)(2,1)} %get-tuple-element.49), channel_id=1, source_target_pairs={{0,2},{1,3},{2,0},{3,1},{4,6},{5,7},{6,4},{7,5},{8,24},{9,25},{10,... | collective-permute-start | bytes 2506760 | tf_op jit(solution)/shard_map/ppermute | solution.py:37
  93.3 10.2 %shard_map.70 = (f32[128,2048]{1,0:T(8,128)}, s16[128,2176]{1,0:T(8,128)(2,1)}, s16[128,2176]{1,0:T(8,128)(2,1)}, s16[128,2176]{1,0:T(8,128)(2,1)}) custom-call(s32[32]{0:T(128)S(1)} %pad_add_fusion.1.table, bf16[384,1024]{1,0:T(8,128)(2,1)} %collective-permute-done.13.refs_0_, bf16[384,1024]{1,0:T(8,128)(2,1)} %collective-permute-done.14.refs_1_, ...), custom_call_target="tpu_custom_call" | custom-call | flops 7283333120 | bytes 1000 | tf_op jit(solution)/shard_map/pallas_call | solution.py:204
  104.1 2.6 %collective-permute-start.16 = (s16[128,2176]{1,0:T(8,128)(2,1)}, s16[128,2176]{1,0:T(8,128)(2,1)}, u32[]{:S(2)}, u32[]{:S(2)}) collective-permute-start(s16[128,2176]{1,0:T(8,128)(2,1)} %get-tuple-element.59), channel_id=1, source_target_pairs={{0,2},{1,3},{2,0},{3,1},{4,6},{5,7},{6,4},{7,5},{8,24},{9,25},{10,... | collective-permute-start | bytes 1671176 | tf_op jit(solution)/shard_map/ppermute | solution.py:37
  107.8 7.7 %shard_map.73 = s16[256,2176]{1,0:T(8,128)(2,1)} custom-call(s32[16]{0:T(128)S(1)} %add.336.table, bf16[256,1024]{1,0:T(8,128)(2,1)S(1)} %copy-done, bf16[128,1024]{1,0:T(8,128)(2,1)S(1)} %collective-permute-done.21.refs_1_, bf16[128,1024]{1,0:T(8,128)(2,1)S(1)} %collective-permute-done.22.refs_2_, bf16[2048,1024]{1,0:T(8,128)(2,1)} %get-tuple-element.43.refs_2_.refs_3_, ...), custom_call_target="tpu_custom_call" | custom-call | flops 4216666624 | bytes 1000 | tf_op jit(solution)/shard_map/pallas_call | solution.py:204
  115.6 5.6 %all-to-all-start = ((s16[16,16,2176]{2,1,0:T(8,128)(2,1)}), s16[16,16,2176]{2,1,0:T(8,128)(2,1)S(1)}, u32[]{:S(2)}, u32[]{:S(2)}) async-start(s16[16,16,2176]{2,1,0:T(8,128)(2,1)} %bitcast.28), calls=%async_computation | async-start | bytes 2228224 | tf_op jit(solution)/shard_map/all_to_all | solution.py:376
  123.8 3.0 %shard_map.68 = (f32[48,2048]{1,0:T(8,128)S(1)}, s16[48,2176]{1,0:T(8,128)(2,1)S(1)}, s16[48,2176]{1,0:T(8,128)(2,1)S(1)}, s16[48,2176]{1,0:T(8,128)(2,1)S(1)}) custom-call(s32[8]{0:T(128)S(1)} %pad_add_fusion.table, f32[192,2048]{1,0:T(8,128)S(1)} %copy-done.10, s16[192,2176]{1,0:T(8,128)(2,1)S(1)} %copy-done.8, ...), custom_call_target="tpu_custom_call" | custom-call | flops 2644999936 | bytes 1000 | tf_op jit(solution)/shard_map/pallas_call | solution.py:251
  128.2 2.4 %collective-permute-start.11 = (s16[48,2176]{1,0:T(8,128)(2,1)S(1)}, s16[48,2176]{1,0:T(8,128)(2,1)S(1)}, u32[]{:S(2)}, u32[]{:S(2)}) collective-permute-start(s16[48,2176]{1,0:T(8,128)(2,1)S(1)} %get-tuple-element.53), channel_id=1, source_target_pairs={{0,16},{1,17},{2,18},{3,19},{4,20},{5,21},{6,22},{7,23},{8,10},{9,... | collective-permute-start | bytes 626696 | tf_op jit(solution)/shard_map/ppermute | solution.py:37
  131.8 2.5 %shard_map.71 = (f32[32,2048]{1,0:T(8,128)S(1)}, s16[32,2176]{1,0:T(8,128)(2,1)S(1)}, s16[32,2176]{1,0:T(8,128)(2,1)S(1)}, s16[32,2176]{1,0:T(8,128)(2,1)S(1)}) custom-call(s32[8]{0:T(128)S(1)} %pad_add_fusion.table, f32[128,2048]{1,0:T(8,128)S(1)} %copy-done.11, s16[128,2176]{1,0:T(8,128)(2,1)} %collective-permute-done.15.one, ...), custom_call_target="tpu_custom_call" | custom-call | flops 2644999936 | bytes 1000 | tf_op jit(solution)/shard_map/pallas_call | solution.py:251
  135.6 5.6 %collective-permute-done.10.one = s16[48,2176]{1,0:T(8,128)(2,1)S(1)} collective-permute-done((s16[48,2176]{1,0:T(8,128)(2,1)S(1)}, s16[48,2176]{1,0:T(8,128)(2,1)S(1)}, u32[]{:S(2)}, u32[]{:S(2)}) %collective-permute-start.10) | collective-permute-done | bytes 208928 | tf_op jit(solution)/shard_map/ppermute | solution.py:37
  144.6 2.9 %collective-permute-done.19.two = s16[32,2176]{1,0:T(8,128)(2,1)S(1)} collective-permute-done((s16[32,2176]{1,0:T(8,128)(2,1)S(1)}, s16[32,2176]{1,0:T(8,128)(2,1)S(1)}, u32[]{:S(2)}, u32[]{:S(2)}) %collective-permute-start.19) | collective-permute-done | bytes 139296 | tf_op jit(solution)/shard_map/ppermute | solution.py:37
  148.9 2.4 %collective-permute-start.23 = (f32[64,2048]{1,0:T(8,128)S(1)}, f32[64,2048]{1,0:T(8,128)S(1)}, u32[]{:S(2)}, u32[]{:S(2)}) collective-permute-start(f32[64,2048]{1,0:T(8,128)S(1)} %get-tuple-element.68), channel_id=1, source_target_pairs={{0,8},{1,9},{2,10},{3,11},{4,12},{5,13},{6,14},{7,15},{8,0},{9,1},... | collective-permute-start | bytes 1572872 | tf_op jit(solution)/shard_map/ppermute | solution.py:37
  (125 shorter events, 38.3 us)
Async XLA Ops:
  0.0 14.7 %collective-permute-start.4 = (bf16[2048,1024]{1,0:T(8,128)(2,1)}, bf16[2048,1024]{1,0:T(8,128)(2,1)}, u32[]{:S(2)}, u32[]{:S(2)}) collective-permute-start(bf16[2048,1024]{1,0:T(8,128)(2,1)} %own.1), channel_id=1, source_target_pairs={{0,8},{1,9},{2,10},{3,11},{4,12},{5,13},{6,14},{7,15},{8,0},{9,1},... | collective-permute-start | bytes 12582920 | tf_op jit(solution)/shard_map/ppermute | solution.py:37
  6.3 8.4 %collective-permute-start.3 = (s32[16,8]{1,0:T(8,128)S(1)}, s32[16,8]{1,0:T(8,128)S(1)}, u32[]{:S(2)}, u32[]{:S(2)}) collective-permute-start(s32[16,8]{1,0:T(8,128)S(1)} %copy.7), channel_id=1, source_target_pairs={{0,8},{1,9},{2,10},{3,11},{4,12},{5,13},{6,14},{7,15},{8,0},{9,1},... | collective-permute-start | bytes 1544 | tf_op jit(solution)/shard_map/ppermute | solution.py:37
  10.8 24.8 %collective-permute-start.2 = (bf16[512,1024]{1,0:T(8,128)(2,1)S(1)}, bf16[512,1024]{1,0:T(8,128)(2,1)S(1)}, u32[]{:S(2)}, u32[]{:S(2)}) collective-permute-start(bf16[512,1024]{1,0:T(8,128)(2,1)S(1)} %pad_maximum_fusion.4.refs_2_), channel_id=1, source_target_pairs={{0,96},{1,97},{2,98},{3,99},{4,100},{5,101},{6,102},{7,103},{8,104... | collective-permute-start | bytes 3145736 | tf_op jit(solution)/shard_map/ppermute | solution.py:37
  13.4 25.3 %collective-permute-start.1 = (bf16[512,1024]{1,0:T(8,128)(2,1)S(1)}, bf16[512,1024]{1,0:T(8,128)(2,1)S(1)}, u32[]{:S(2)}, u32[]{:S(2)}) collective-permute-start(bf16[512,1024]{1,0:T(8,128)(2,1)S(1)} %pad_maximum_fusion.4.refs_2_), channel_id=1, source_target_pairs={{0,32},{1,33},{2,34},{3,35},{4,36},{5,37},{6,38},{7,39},{8,40},{9,... | collective-permute-start | bytes 3145736 | tf_op jit(solution)/shard_map/ppermute | solution.py:37
  40.3 23.4 %collective-permute-start.6 = (bf16[512,1024]{1,0:T(8,128)(2,1)}, bf16[512,1024]{1,0:T(8,128)(2,1)}, u32[]{:S(2)}, u32[]{:S(2)}) collective-permute-start(bf16[512,1024]{1,0:T(8,128)(2,1)} %get-tuple-element.75), channel_id=1, source_target_pairs={{0,96},{1,97},{2,98},{3,99},{4,100},{5,101},{6,102},{7,103},{8,104... | collective-permute-start | bytes 3145736 | tf_op jit(solution)/shard_map/ppermute | solution.py:37
  40.6 24.7 %collective-permute-start.5 = (bf16[512,1024]{1,0:T(8,128)(2,1)}, bf16[512,1024]{1,0:T(8,128)(2,1)}, u32[]{:S(2)}, u32[]{:S(2)}) collective-permute-start(bf16[512,1024]{1,0:T(8,128)(2,1)} %get-tuple-element.76), channel_id=1, source_target_pairs={{0,32},{1,33},{2,34},{3,35},{4,36},{5,37},{6,38},{7,39},{8,40},{9,... | collective-permute-start | bytes 3145736 | tf_op jit(solution)/shard_map/ppermute | solution.py:37
  51.7 63.9 %all-to-all-start.1 = ((s16[16,32,2176]{2,1,0:T(8,128)(2,1)}), s16[16,32,2176]{2,1,0:T(8,128)(2,1)S(1)}, u32[]{:S(2)}, u32[]{:S(2)}) async-start(s16[16,32,2176]{2,1,0:T(8,128)(2,1)} %bitcast.25), calls=%async_computation.1 | async-start | bytes 4456448 | tf_op jit(solution)/shard_map/all_to_all | solution.py:376
  69.6 19.1 %collective-permute-start.14 = (bf16[384,1024]{1,0:T(8,128)(2,1)}, bf16[384,1024]{1,0:T(8,128)(2,1)}, u32[]{:S(2)}, u32[]{:S(2)}) collective-permute-start(bf16[384,1024]{1,0:T(8,128)(2,1)} %get-tuple-element.73), channel_id=1, source_target_pairs={{0,96},{1,97},{2,98},{3,99},{4,100},{5,101},{6,102},{7,103},{8,104... | collective-permute-start | bytes 2359304 | tf_op jit(solution)/shard_map/ppermute | solution.py:37
  69.9 18.8 %collective-permute-start.13 = (bf16[384,1024]{1,0:T(8,128)(2,1)}, bf16[384,1024]{1,0:T(8,128)(2,1)}, u32[]{:S(2)}, u32[]{:S(2)}) collective-permute-start(bf16[384,1024]{1,0:T(8,128)(2,1)} %get-tuple-element.74), channel_id=1, source_target_pairs={{0,32},{1,33},{2,34},{3,35},{4,36},{5,37},{6,38},{7,39},{8,40},{9,... | collective-permute-start | bytes 2359304 | tf_op jit(solution)/shard_map/ppermute | solution.py:37
  83.4 23.3 %collective-permute-start.7 = (s16[192,2176]{1,0:T(8,128)(2,1)}, s16[192,2176]{1,0:T(8,128)(2,1)S(1)}, u32[]{:S(2)}, u32[]{:S(2)}) collective-permute-start(s16[192,2176]{1,0:T(8,128)(2,1)} %get-tuple-element.48), channel_id=1, source_target_pairs={{0,1},{1,2},{2,3},{3,0},{4,5},{5,6},{6,7},{7,4},{8,12},{9,13},{10,... | collective-permute-start | bytes 2506760 | tf_op jit(solution)/shard_map/ppermute | solution.py:37
  85.0 36.2 %collective-permute-start.8 = (s16[192,2176]{1,0:T(8,128)(2,1)}, s16[192,2176]{1,0:T(8,128)(2,1)}, u32[]{:S(2)}, u32[]{:S(2)}) collective-permute-start(s16[192,2176]{1,0:T(8,128)(2,1)} %get-tuple-element.49), channel_id=1, source_target_pairs={{0,2},{1,3},{2,0},{3,1},{4,6},{5,7},{6,4},{7,5},{8,24},{9,25},{10,... | collective-permute-start | bytes 2506760 | tf_op jit(solution)/shard_map/ppermute | solution.py:37
  87.6 33.6 %collective-permute-start.9 = (s16[192,2176]{1,0:T(8,128)(2,1)}, s16[192,2176]{1,0:T(8,128)(2,1)}, u32[]{:S(2)}, u32[]{:S(2)}) collective-permute-start(s16[192,2176]{1,0:T(8,128)(2,1)} %get-tuple-element.50), channel_id=1, source_target_pairs={{0,3},{1,0},{2,1},{3,2},{4,7},{5,4},{6,5},{7,6},{8,28},{9,29},{10,... | collective-permute-start | bytes 2506760 | tf_op jit(solution)/shard_map/ppermute | solution.py:37
  90.7 12.8 %collective-permute-start.22 = (bf16[128,1024]{1,0:T(8,128)(2,1)S(1)}, bf16[128,1024]{1,0:T(8,128)(2,1)S(1)}, u32[]{:S(2)}, u32[]{:S(2)}) collective-permute-start(bf16[128,1024]{1,0:T(8,128)(2,1)S(1)} %slice.61), channel_id=1, source_target_pairs={{0,96},{1,97},{2,98},{3,99},{4,100},{5,101},{6,102},{7,103},{8,104... | collective-permute-start | bytes 786440 | tf_op jit(solution)/shard_map/ppermute | solution.py:37
  92.2 11.9 %collective-permute-start.21 = (bf16[128,1024]{1,0:T(8,128)(2,1)S(1)}, bf16[128,1024]{1,0:T(8,128)(2,1)S(1)}, u32[]{:S(2)}, u32[]{:S(2)}) collective-permute-start(bf16[128,1024]{1,0:T(8,128)(2,1)S(1)} %slice.60), channel_id=1, source_target_pairs={{0,32},{1,33},{2,34},{3,35},{4,36},{5,37},{6,38},{7,39},{8,40},{9,... | collective-permute-start | bytes 786440 | tf_op jit(solution)/shard_map/ppermute | solution.py:37
  103.5 27.2 %collective-permute-start.15 = (s16[128,2176]{1,0:T(8,128)(2,1)}, s16[128,2176]{1,0:T(8,128)(2,1)}, u32[]{:S(2)}, u32[]{:S(2)}) collective-permute-start(s16[128,2176]{1,0:T(8,128)(2,1)} %get-tuple-element.58), channel_id=1, source_target_pairs={{0,1},{1,2},{2,3},{3,0},{4,5},{5,6},{6,7},{7,4},{8,12},{9,13},{10,... | collective-permute-start | bytes 1671176 | tf_op jit(solution)/shard_map/ppermute | solution.py:37
  104.1 27.7 %collective-permute-start.16 = (s16[128,2176]{1,0:T(8,128)(2,1)}, s16[128,2176]{1,0:T(8,128)(2,1)}, u32[]{:S(2)}, u32[]{:S(2)}) collective-permute-start(s16[128,2176]{1,0:T(8,128)(2,1)} %get-tuple-element.59), channel_id=1, source_target_pairs={{0,2},{1,3},{2,0},{3,1},{4,6},{5,7},{6,4},{7,5},{8,24},{9,25},{10,... | collective-permute-start | bytes 1671176 | tf_op jit(solution)/shard_map/ppermute | solution.py:37
  106.7 25.1 %collective-permute-start.17 = (s16[128,2176]{1,0:T(8,128)(2,1)}, s16[128,2176]{1,0:T(8,128)(2,1)}, u32[]{:S(2)}, u32[]{:S(2)}) collective-permute-start(s16[128,2176]{1,0:T(8,128)(2,1)} %get-tuple-element.60), channel_id=1, source_target_pairs={{0,3},{1,0},{2,1},{3,2},{4,7},{5,4},{6,5},{7,6},{8,28},{9,29},{10,... | collective-permute-start | bytes 1671176 | tf_op jit(solution)/shard_map/ppermute | solution.py:37
  115.6 32.2 %all-to-all-start = ((s16[16,16,2176]{2,1,0:T(8,128)(2,1)}), s16[16,16,2176]{2,1,0:T(8,128)(2,1)S(1)}, u32[]{:S(2)}, u32[]{:S(2)}) async-start(s16[16,16,2176]{2,1,0:T(8,128)(2,1)} %bitcast.28), calls=%async_computation | async-start | bytes 2228224 | tf_op jit(solution)/shard_map/all_to_all | solution.py:376
  126.8 14.3 %collective-permute-start.10 = (s16[48,2176]{1,0:T(8,128)(2,1)S(1)}, s16[48,2176]{1,0:T(8,128)(2,1)S(1)}, u32[]{:S(2)}, u32[]{:S(2)}) collective-permute-start(s16[48,2176]{1,0:T(8,128)(2,1)S(1)} %get-tuple-element.52), channel_id=1, source_target_pairs={{0,4},{1,5},{2,6},{3,7},{4,16},{5,17},{6,18},{7,19},{8,9},{9,10},{... | collective-permute-start | bytes 626696 | tf_op jit(solution)/shard_map/ppermute | solution.py:37
  128.2 16.0 %collective-permute-start.11 = (s16[48,2176]{1,0:T(8,128)(2,1)S(1)}, s16[48,2176]{1,0:T(8,128)(2,1)S(1)}, u32[]{:S(2)}, u32[]{:S(2)}) collective-permute-start(s16[48,2176]{1,0:T(8,128)(2,1)S(1)} %get-tuple-element.53), channel_id=1, source_target_pairs={{0,16},{1,17},{2,18},{3,19},{4,20},{5,21},{6,22},{7,23},{8,10},{9,... | collective-permute-start | bytes 626696 | tf_op jit(solution)/shard_map/ppermute | solution.py:37
  130.6 13.6 %collective-permute-start.12 = (s16[48,2176]{1,0:T(8,128)(2,1)S(1)}, s16[48,2176]{1,0:T(8,128)(2,1)S(1)}, u32[]{:S(2)}, u32[]{:S(2)}) collective-permute-start(s16[48,2176]{1,0:T(8,128)(2,1)S(1)} %get-tuple-element.54), channel_id=1, source_target_pairs={{0,20},{1,21},{2,22},{3,23},{4,0},{5,1},{6,2},{7,3},{8,11},{9,8},{... | collective-permute-start | bytes 626696 | tf_op jit(solution)/shard_map/ppermute | solution.py:37
  134.3 10.3 %collective-permute-start.18 = (s16[32,2176]{1,0:T(8,128)(2,1)S(1)}, s16[32,2176]{1,0:T(8,128)(2,1)S(1)}, u32[]{:S(2)}, u32[]{:S(2)}) collective-permute-start(s16[32,2176]{1,0:T(8,128)(2,1)S(1)} %get-tuple-element.62), channel_id=1, source_target_pairs={{0,4},{1,5},{2,6},{3,7},{4,16},{5,17},{6,18},{7,19},{8,9},{9,10},{... | collective-permute-start | bytes 417800 | tf_op jit(solution)/shard_map/ppermute | solution.py:37
  134.6 12.8 %collective-permute-start.19 = (s16[32,2176]{1,0:T(8,128)(2,1)S(1)}, s16[32,2176]{1,0:T(8,128)(2,1)S(1)}, u32[]{:S(2)}, u32[]{:S(2)}) collective-permute-start(s16[32,2176]{1,0:T(8,128)(2,1)S(1)} %get-tuple-element.63), channel_id=1, source_target_pairs={{0,16},{1,17},{2,18},{3,19},{4,20},{5,21},{6,22},{7,23},{8,10},{9,... | collective-permute-start | bytes 417800 | tf_op jit(solution)/shard_map/ppermute | solution.py:37
  141.1 6.3 %collective-permute-start.20 = (s16[32,2176]{1,0:T(8,128)(2,1)S(1)}, s16[32,2176]{1,0:T(8,128)(2,1)S(1)}, u32[]{:S(2)}, u32[]{:S(2)}) collective-permute-start(s16[32,2176]{1,0:T(8,128)(2,1)S(1)} %get-tuple-element.64), channel_id=1, source_target_pairs={{0,20},{1,21},{2,22},{3,23},{4,0},{5,1},{6,2},{7,3},{8,11},{9,8},{... | collective-permute-start | bytes 417800 | tf_op jit(solution)/shard_map/ppermute | solution.py:37
  (28 other events, 115.9 us)
